TPU v7x, 128 devices: a whole 4x4x4 slice. The times are simulated.
128 devices in a mesh: seq: 64 (over z, y_hi, x, core), utt: 2 (over y_lo).
Axes of the slice: x: 4, y: 4 (y_hi: 2, y_lo: 2; y = y_hi * 2 + y_lo), z: 4, core: 2. Of those that a mesh axis runs over, the one named last changes fastest.
Arguments:
- inputs: bfloat16 [2, 8192, 1536], P('utt', 'seq'), may hold values from -6 to 6
- attention_norm_gain: float32 [1536], replicated, may hold values from 1.5 to 5.5
- w_query: bfloat16 [1536, 768], replicated, may hold values from -0.15625 to 0.15625
- w_key: bfloat16 [1536, 768], replicated, may hold values from -0.15625 to 0.15625
- w_value: bfloat16 [1536, 768], replicated, may hold values from -0.15625 to 0.15625
- w_out: bfloat16 [768, 1536], replicated, may hold values from -0.21875 to 0.21875
- gain_conv: float32 [1536], replicated, may hold values from 0.25 to 1.75
- kernel: float32 [32, 1536], replicated, may hold values from -1 to 1
- w_point: bfloat16 [1536, 1536], replicated, may hold values from -0.15625 to 0.15625
- cotangent: bfloat16 [2, 8192, 1536], P('utt', 'seq'), may hold values from -6 to 6
Outputs:
- layer_out: bfloat16 [2, 8192, 1536], P('utt', 'seq')
- grad_hidden: bfloat16 [2, 8192, 1536], P('utt', 'seq')
- grad_point: float32 [1536, 1536], P('seq')
- grad_kernel: float32 [32, 1536], replicated
- grad_gain: float32 [1536], replicated
All inputs are finite; a program needn't handle non-finite values.
Results may differ from a plain program's by a relative error of at most 0.02.
The roundings to bfloat16 on the way count: a program that leaves them out, or rounds other values in their place, can miss the bound.
Values may be sent and summed in bfloat16 or wider, within the bound.
A program may use at most 192 MiB of HBM per device.

v0:
```python
import math

import jax
import jax.numpy as jnp
from jax import lax
from jax.sharding import PartitionSpec as P

D = 1536
HEADS = 8
HEAD_DIM = 96
KER = 32


def with_halo(block, sides, width):
    for axis, dim in sides:
        count = lax.axis_size(axis)
        forward = [(i, i + 1) for i in range(count - 1)]
        backward = [(target, source) for source, target in forward]
        low = lax.ppermute(
            lax.slice_in_dim(block, block.shape[dim] - width, None, axis=dim), axis, forward
        )
        high = lax.ppermute(lax.slice_in_dim(block, 0, width, axis=dim), axis, backward)
        block = jnp.concatenate([low, block, high], axis=dim)
    return block


def standardize_rows(values):
    mean = jnp.mean(values, axis=-1, keepdims=True)
    centered = values - mean
    rstd = lax.rsqrt(jnp.mean(centered * centered, axis=-1, keepdims=True) + 1e-05)
    return (centered * rstd, rstd)


def attend_piece(carry, key_rows, value_rows, query_heads):
    running, total, accum = carry
    count = key_rows.shape[0]
    key_heads = key_rows.reshape(count, HEADS, HEAD_DIM)
    value_heads = value_rows.reshape(count, HEADS, HEAD_DIM)
    scores = jnp.einsum("thd,fhd->htf", query_heads, key_heads, preferred_element_type=jnp.float32)
    scores = scores * (1.0 / math.sqrt(HEAD_DIM))
    newest = jnp.maximum(running, jnp.max(scores, axis=-1))
    factor = jnp.exp(running - newest)
    expo = jnp.exp(scores - newest[:, :, None])
    total = jnp.sum(expo, axis=-1)
    summed = jnp.einsum(
        "htf,fhd->thd", expo.astype(jnp.bfloat16), value_heads, preferred_element_type=jnp.float32
    )
    accum = accum * factor.T[:, :, None] + summed
    return (newest, total, accum)


def depthwise(source, kernel, count):
    result = jnp.zeros((count, source.shape[1]), jnp.float32)
    for tap in range(kernel.shape[0]):
        result = result + kernel[tap] * source[tap : tap + count].astype(jnp.float32)
    return result


def swish_grad(values):
    sig = jax.nn.sigmoid(values)
    return sig * (1.0 + values * (1.0 - sig))


def on_device(
    inputs,
    attention_norm_gain,
    w_query,
    w_key,
    w_value,
    w_out,
    gain_conv,
    kernel,
    w_point,
    cotangent,
):
    input_rows = inputs[0].astype(jnp.float32)
    count = input_rows.shape[0]
    width = D
    half = KER // 2
    standardized_input, unused_item = standardize_rows(input_rows)
    normed_rows = (standardized_input * attention_norm_gain).astype(jnp.bfloat16)
    query_heads = (
        jnp.dot(normed_rows, w_query, preferred_element_type=jnp.float32)
        .astype(jnp.bfloat16)
        .reshape(count, HEADS, HEAD_DIM)
    )
    start_carry = (
        jnp.full((HEADS, count), -1e30, jnp.float32),
        jnp.zeros((HEADS, count), jnp.float32),
        jnp.zeros((count, HEADS, HEAD_DIM), jnp.float32),
    )
    keys = jnp.dot(normed_rows, w_key, preferred_element_type=jnp.float32).astype(jnp.bfloat16)
    values = jnp.dot(normed_rows, w_value, preferred_element_type=jnp.float32).astype(jnp.bfloat16)
    carry = attend_piece(
        start_carry,
        lax.all_gather(keys, "seq", axis=0, tiled=True),
        lax.all_gather(values, "seq", axis=0, tiled=True),
        query_heads,
    )
    mixed = (
        (carry[2] / carry[1].T[:, :, None]).reshape(count, HEADS * HEAD_DIM).astype(jnp.bfloat16)
    )
    hidden_f = (
        (input_rows + jnp.dot(mixed, w_out, preferred_element_type=jnp.float32))
        .astype(jnp.bfloat16)
        .astype(jnp.float32)
    )
    hhat, rstd = standardize_rows(hidden_f)
    conv_in = (hhat * gain_conv).astype(jnp.bfloat16)
    grad_now = cotangent[0]
    taps_source = with_halo(conv_in, (("seq", 0),), half)
    conv = depthwise(taps_source, kernel, count)
    back = lax.dot_general(
        grad_now, w_point, (((1,), (1,)), ((), ())), preferred_element_type=jnp.float32
    )
    dz = back * swish_grad(conv)
    dz_pad = with_halo(dz.astype(jnp.bfloat16), (("seq", 0),), half).astype(dz.dtype)
    act = (conv * jax.nn.sigmoid(conv)).astype(jnp.bfloat16)
    layer_out = (hidden_f + jnp.dot(act, w_point, preferred_element_type=jnp.float32)).astype(
        jnp.bfloat16
    )
    taps_f = taps_source.astype(jnp.float32)
    local_kernel = jnp.stack(
        [jnp.sum(dz * taps_f[tap : tap + count], axis=0) for tap in range(KER)]
    )
    dconv_in = jnp.zeros((count, width), jnp.float32)
    for tap in range(KER):
        dconv_in = dconv_in + kernel[tap] * dz_pad[2 * half - tap : 2 * half - tap + count]
    local_gain = jnp.sum(dconv_in * hhat, axis=0)
    scaled = dconv_in * gain_conv
    inner = (
        scaled
        - jnp.mean(scaled, axis=-1, keepdims=True)
        - hhat * jnp.mean(scaled * hhat, axis=-1, keepdims=True)
    )
    grad_hidden = (grad_now.astype(jnp.float32) + rstd * inner).astype(jnp.bfloat16)
    grad_scale = 1.0 / math.sqrt(lax.axis_size("utt") * lax.axis_size("seq") * count)
    summed_kernel, summed_gain = lax.psum((local_kernel, local_gain), ("seq", "utt"))
    shares = lax.psum_scatter(
        lax.dot_general(
            act, grad_now, (((0,), (0,)), ((), ())), preferred_element_type=jnp.float32
        ),
        "seq",
        scatter_dimension=0,
        tiled=True,
    )
    grad_point = lax.psum(shares.astype(jnp.bfloat16), "utt").astype(jnp.float32)
    return (
        layer_out[None],
        grad_hidden[None],
        grad_point * grad_scale,
        summed_kernel * grad_scale,
        summed_gain * grad_scale,
    )


def solution(mesh):
    placed = (P("utt", "seq", None), P(), P(), P(), P(), P(), P(), P(), P(), P("utt", "seq", None))
    return jax.shard_map(
        on_device,
        mesh=mesh,
        in_specs=placed,
        out_specs=(P("utt", "seq", None), P("utt", "seq", None), P("seq", None), P(), P()),
        check_vma=False,
    )
```

profile of v0, /device:TPU:1, one launch (start us, length us, event | category | flops | bytes accessed | tf_op | source)
XLA Modules:
  0.0 621.9 jit_solution(4490849735705816869)
XLA Ops:
  9.8 3.0 convolution_convert_fusion.1
  12.9 3.0 convolution_convert_fusion
  16.0 2.3 convolution_convert_fusion.2
  18.5 2.5 slice_reduce_fusion.31
  21.0 89.4 %all-gather.3.cloned.1.call-done = bf16[8192,768]{1,0:T(8,128)(2,1)} async-done(((bf16[128,768]{1,0:T(8,128)(2,1)}), bf16[8192,768]{1,0:T(8,128)(2,1)}) %all-gather.3.cloned.1.call-update) | async-done | bytes 12582928 | tf_op jit(solution)/shard_map/all_gather | solution.py:96
  110.4 16.6 %copy.19 = bf16[8192,768]{0,1:T(8,128)(2,1)} copy(bf16[8192,768]{1,0:T(8,128)(2,1)} %all-gather.3.cloned.1.call-done) | data formatting | bytes 25165824 | tf_op jit(solution)/shard_map/all_gather | solution.py:96
  127.0 16.2 %multiply_reduce_fusion = (f32[8,128]{1,0:T(8,128)S(1)}, f32[8,128,8192]{2,1,0:T(8,128)}) fusion(bf16[128,8,96]{0,2,1:T(8,128)(2,1)S(1)} %bitcast.59, bf16[8192,8,96]{0,2,1:T(8,128)(2,1)} %bitcast.57), kind=kOutput, calls=%fused_computation.1 | convolution fusion | flops 1627388928 | bytes 46338048 | tf_op jit(solution)/shard_map/thd,fhd->htf/dot_general | solution.py:39
  143.2 14.2 %fusion = f32[8,128]{1,0:T(8,128)S(1)} fusion(f32[8,128,8192]{2,1,0:T(8,128)} %get-tuple-element.81, f32[8,128]{1,0:T(8,128)S(1)} %get-tuple-element.79), kind=kLoop, calls=%fused_computation.2 | loop fusion | flops 25164800 | bytes 33562624 | tf_op jit(solution)/shard_map/reduce_sum | solution.py:44
  157.4 48.4 %all-gather.5.cloned.1.call-done = bf16[8192,768]{1,0:T(8,128)(2,1)} async-done(((bf16[128,768]{1,0:T(8,128)(2,1)}), bf16[8192,768]{1,0:T(8,128)(2,1)}) %all-gather.5.cloned.1.call-update) | async-done | bytes 12582928 | tf_op jit(solution)/shard_map/all_gather | solution.py:97
  205.8 16.6 %copy.20 = bf16[8192,768]{0,1:T(8,128)(2,1)} copy(bf16[8192,768]{1,0:T(8,128)(2,1)} %all-gather.5.cloned.1.call-done) | data formatting | bytes 25165824 | tf_op jit(solution)/shard_map/all_gather | solution.py:97
  222.6 17.0 %fusion.19 = bf16[128,8,96]{0,2,1:T(8,128)(2,1)S(1)} fusion(bf16[8192,8,96]{0,2,1:T(8,128)(2,1)} %bitcast.56, f32[8,128,8192]{2,1,0:T(8,128)} %get-tuple-element.81, f32[8,128]{1,0:T(8,128)S(1)} %get-tuple-element.79, f32[128,8]{0,1:T(8,128)S(1)} %bitcast.60, f32[128,8]{0,1:T(8,128)S(1)} %get-tuple-element.78), kind=kOutput, calls=%fused_computation.49 | convolution fusion | flops 1636073472 | bytes 46346240 | tf_op jit(solution)/shard_map/htf,fhd->thd/dot_general | solution.py:45
  241.0 3.2 collective-permute-start
  244.2 2.1 collective-permute-start.1
  246.3 1.5 slice_reduce_fusion.30
  248.0 1.6 collective-permute-done.1
  249.8 3.8 multiply_add_fusion
  254.6 5.1 fusion.121
  260.7 6.3 %fusion.28 = (f32[1536]{0:T(1024)S(1)}, f32[1536]{0:T(1024)S(1)}, f32[1536]{0:T(1024)S(1)}, f32[1536]{0:T(1024)S(1)}, f32[1536]{0:T(1024)S(1)}, /*index=5*/f32[1...) fusion(f32[160,1536]{1,0:T(8,128)S(1)} %maximum_convert_fusion., ...), kind=kOutput, calls=%fused_computation.59 | convolution fusion | flops 612799488 | bytes 21344256 | tf_op jit(solution)/shard_map/dot_general | solution.py:113
  267.6 2.6 collective-permute-start.2
  270.2 2.3 collective-permute-start.3
  272.6 1.5 fusion.46
  274.1 4.1 fusion.9
  297.3 6.0 stack.131
  304.4 7.4 %multiply_reduce_fusion.1 = (f32[1536]{0:T(1024)}, f32[128]{0:T(128)}, f32[128]{0:T(128)}, f32[128,1536]{1,0:T(8,128)}) fusion(f32[128,1536]{1,0:T(8,128)S(1)} %get-tuple-element.83, f32[128]{0:T(128)} %copy-done.41, f32[128]{0:T(128)} %copy-done.40, f32[1536]{0:T(1024)S(1)} %copy-done.8, f32[160,1536]{1,0:T(8,128)S(1)} %maximum_convert_fusion, ...), kind=kLoop, calls=%fused_computation.185 | loop fusion | flops 13957376 | bytes 26949632 | tf_op jit(solution)/shard_map/reduce_sum | solution.py:129
  311.8 73.4 %psum.23 = f32[1536]{0:T(1024)S(1)} all-reduce(f32[1536]{0:T(1024)} %get-tuple-element.37), channel_id=1, replica_groups=mesh['seq'=64,'utt'=2] {'seq','utt'}, use_global_device_ids=true, to_apply=%region_44.0 | all-reduce | flops 1536 | bytes 12288 | tf_op jit(solution)/shard_map/psum | solution.py:138
  385.9 2.3 fusion.91
  388.7 49.7 %reduce-scatter.2.cloned.1.call-done = f32[24,1536]{1,0:T(8,128)} async-done(((f32[1536,1536]{1,0:T(8,128)}), f32[24,1536]{1,0:T(8,128)}) %reduce-scatter.2.cloned.1.call-update) | async-done | bytes 147472 | tf_op jit(solution)/shard_map/reduce_scatter | solution.py:139
  438.4 1.6 convert_element_type.209
  440.0 145.8 %all-reduce.5.cloned.1.call-done = f32[32,1536]{1,0:T(8,128)} async-done(((f32[32,1536]{1,0:T(8,128)}), f32[32,1536]{1,0:T(8,128)}) %all-reduce.5.cloned.1.call-update) | async-done | bytes 196624 | tf_op jit(solution)/shard_map/psum | solution.py:138
  585.8 1.6 broadcast_multiply_fusion
  587.4 26.5 %all-reduce.3.cloned.1.call-done = bf16[24,1536]{1,0:T(8,128)(2,1)} async-done(((bf16[24,1536]{1,0:T(8,128)(2,1)}), bf16[24,1536]{1,0:T(8,128)(2,1)}) %all-reduce.3.cloned.1.call-update) | async-done | bytes 73744 | tf_op jit(solution)/shard_map/psum | solution.py:147
  613.8 1.6 convert_multiply_fusion
  (146 shorter events, 28.2 us)
Async XLA Ops:
  7.2 232.4 %copy-start = (bf16[768,1536]{1,0:T(8,128)(2,1)S(1)}, bf16[768,1536]{1,0:T(8,128)(2,1)}, u32[]{:S(2)}) copy-start(bf16[768,1536]{1,0:T(8,128)(2,1)} %param.15) | copy-start | bytes 7077892
  7.2 103.2 %all-gather.3.cloned.1.call-start = ((), (), s32[]{:S(2)}) async-start(), calls=%async_computation.1 | async-start | bytes 12779520 | tf_op jit(solution)/shard_map/all_gather | solution.py:96
  12.8 192.9 %all-gather.5.cloned.1.call-start = ((), (), s32[]{:S(2)}) async-start(), calls=%async_computation.2 | async-start | bytes 12779520 | tf_op jit(solution)/shard_map/all_gather | solution.py:97
  15.9 422.5 %reduce-scatter.2.cloned.1.call-start = ((), (), s32[]{:S(2)}) async-start(), calls=%async_computation.3 | async-start | bytes 9584640 | tf_op jit(solution)/shard_map/reduce_scatter | solution.py:139
  222.4 17.2 %copy-start.3 = (bf16[1,128,1536]{2,1,0:T(8,128)(2,1)S(1)}, bf16[1,128,1536]{2,1,0:T(8,128)(2,1)}, u32[]{:S(2)}) copy-start(bf16[1,128,1536]{2,1,0:T(8,128)(2,1)} %param.10) | copy-start | bytes 1179652
  222.4 18.1 %copy-start.8 = (f32[1536]{0:T(1024)S(1)}, f32[1536]{0:T(1024)}, u32[]{:S(2)}) copy-start(f32[1536]{0:T(1024)} %param.16) | copy-start | bytes 18436
  222.4 27.2 %copy-start.9 = (f32[1536]{0:T(1024)S(1)}, f32[1536]{0:T(1024)}, u32[]{:S(2)}) copy-start(f32[1536]{0:T(1024)} %get-tuple-element.41) | copy-start | bytes 18436
  222.4 27.2 %copy-start.10 = (f32[1536]{0:T(1024)S(1)}, f32[1536]{0:T(1024)}, u32[]{:S(2)}) copy-start(f32[1536]{0:T(1024)} %get-tuple-element.42) | copy-start | bytes 18436
  222.4 27.2 %copy-start.11 = (f32[1536]{0:T(1024)S(1)}, f32[1536]{0:T(1024)}, u32[]{:S(2)}) copy-start(f32[1536]{0:T(1024)} %get-tuple-element.43) | copy-start | bytes 18436
  222.4 27.2 %copy-start.12 = (f32[1536]{0:T(1024)S(1)}, f32[1536]{0:T(1024)}, u32[]{:S(2)}) copy-start(f32[1536]{0:T(1024)} %get-tuple-element.44) | copy-start | bytes 18436
  222.4 27.2 %copy-start.13 = (f32[1536]{0:T(1024)S(1)}, f32[1536]{0:T(1024)}, u32[]{:S(2)}) copy-start(f32[1536]{0:T(1024)} %get-tuple-element.45) | copy-start | bytes 18436
  222.4 27.2 %copy-start.14 = (f32[1536]{0:T(1024)S(1)}, f32[1536]{0:T(1024)}, u32[]{:S(2)}) copy-start(f32[1536]{0:T(1024)} %get-tuple-element.46) | copy-start | bytes 18436
  222.4 27.2 %copy-start.15 = (f32[1536]{0:T(1024)S(1)}, f32[1536]{0:T(1024)}, u32[]{:S(2)}) copy-start(f32[1536]{0:T(1024)} %get-tuple-element.47) | copy-start | bytes 18436
  222.5 27.2 %copy-start.16 = (f32[1536]{0:T(1024)S(1)}, f32[1536]{0:T(1024)}, u32[]{:S(2)}) copy-start(f32[1536]{0:T(1024)} %get-tuple-element.48) | copy-start | bytes 18436
  222.5 27.2 %copy-start.17 = (f32[1536]{0:T(1024)S(1)}, f32[1536]{0:T(1024)}, u32[]{:S(2)}) copy-start(f32[1536]{0:T(1024)} %get-tuple-element.49) | copy-start | bytes 18436
  222.5 27.2 %copy-start.18 = (f32[1536]{0:T(1024)S(1)}, f32[1536]{0:T(1024)}, u32[]{:S(2)}) copy-start(f32[1536]{0:T(1024)} %get-tuple-element.50) | copy-start | bytes 18436
  222.5 27.2 %copy-start.19 = (f32[1536]{0:T(1024)S(1)}, f32[1536]{0:T(1024)}, u32[]{:S(2)}) copy-start(f32[1536]{0:T(1024)} %get-tuple-element.51) | copy-start | bytes 18436
  222.5 27.2 %copy-start.20 = (f32[1536]{0:T(1024)S(1)}, f32[1536]{0:T(1024)}, u32[]{:S(2)}) copy-start(f32[1536]{0:T(1024)} %get-tuple-element.52) | copy-start | bytes 18436
  222.5 27.2 %copy-start.21 = (f32[1536]{0:T(1024)S(1)}, f32[1536]{0:T(1024)}, u32[]{:S(2)}) copy-start(f32[1536]{0:T(1024)} %get-tuple-element.53) | copy-start | bytes 18436
  222.5 27.2 %copy-start.22 = (f32[1536]{0:T(1024)S(1)}, f32[1536]{0:T(1024)}, u32[]{:S(2)}) copy-start(f32[1536]{0:T(1024)} %get-tuple-element.54) | copy-start | bytes 18436
  222.5 27.2 %copy-start.23 = (f32[1536]{0:T(1024)S(1)}, f32[1536]{0:T(1024)}, u32[]{:S(2)}) copy-start(f32[1536]{0:T(1024)} %get-tuple-element.55) | copy-start | bytes 18436
  222.5 27.2 %copy-start.24 = (f32[1536]{0:T(1024)S(1)}, f32[1536]{0:T(1024)}, u32[]{:S(2)}) copy-start(f32[1536]{0:T(1024)} %get-tuple-element.56) | copy-start | bytes 18436
  222.5 27.2 %copy-start.25 = (f32[1536]{0:T(1024)S(1)}, f32[1536]{0:T(1024)}, u32[]{:S(2)}) copy-start(f32[1536]{0:T(1024)} %get-tuple-element.57) | copy-start | bytes 18436
  222.6 27.2 %copy-start.26 = (f32[1536]{0:T(1024)S(1)}, f32[1536]{0:T(1024)}, u32[]{:S(2)}) copy-start(f32[1536]{0:T(1024)} %get-tuple-element.58) | copy-start | bytes 18436
  222.6 32.1 %copy-start.4 = (bf16[1,128,1536]{2,1,0:T(8,128)(2,1)S(1)}, bf16[1,128,1536]{2,1,0:T(8,128)(2,1)}, u32[]{:S(2)}) copy-start(bf16[1,128,1536]{2,1,0:T(8,128)(2,1)} %param.19) | copy-start | bytes 1179652
  241.0 7.0 %collective-permute-start = (bf16[16,1536]{1,0:T(8,128)(2,1)S(1)}, bf16[16,1536]{1,0:T(8,128)(2,1)S(1)}, u32[]{:S(2)}, u32[]{:S(2)}) collective-permute-start(bf16[16,1536]{1,0:T(8,128)(2,1)S(1)} %get-tuple-element.76), channel_id=1, source_target_pairs={{0,2},{2,4},{4,6},{6,8},{8,10},{10,12},{12,14},{14,16},{16,18},{18... | collective-permute-start | bytes 147464 | tf_op jit(solution)/shard_map/ppermute | solution.py:19
  244.2 5.4 collective-permute-start.1
  259.7 326.0 %all-reduce.5.cloned.1.call-start = ((), (), s32[]{:S(2)}) async-start(), calls=%async_computation.5 | async-start | bytes 393216 | tf_op jit(solution)/shard_map/psum | solution.py:138
  267.6 35.8 %collective-permute-start.2 = (bf16[16,1536]{1,0:T(8,128)(2,1)}, bf16[16,1536]{1,0:T(8,128)(2,1)}, u32[]{:S(2)}, u32[]{:S(2)}) collective-permute-start(bf16[16,1536]{1,0:T(8,128)(2,1)} %get-tuple-element.74), channel_id=1, source_target_pairs={{0,2},{2,4},{4,6},{6,8},{8,10},{10,12},{12,14},{14,16},{16,18},{18... | collective-permute-start | bytes 147464 | tf_op jit(solution)/shard_map/ppermute | solution.py:19
  270.2 33.2 %collective-permute-start.3 = (bf16[16,1536]{1,0:T(8,128)(2,1)}, bf16[16,1536]{1,0:T(8,128)(2,1)}, u32[]{:S(2)}, u32[]{:S(2)}) collective-permute-start(bf16[16,1536]{1,0:T(8,128)(2,1)} %get-tuple-element.75), channel_id=1, source_target_pairs={{2,0},{4,2},{6,4},{8,6},{10,8},{12,10},{14,12},{16,14},{18,16},{20... | collective-permute-start | bytes 147464 | tf_op jit(solution)/shard_map/ppermute | solution.py:22
  303.4 310.5 %all-reduce.3.cloned.1.call-start = ((), (), s32[]{:S(2)}) async-start(), calls=%async_computation.4 | async-start | bytes 147456 | tf_op jit(solution)/shard_map/psum | solution.py:147
  304.4 81.5 %copy-start.5 = (bf16[1,128,1536]{2,1,0:T(8,128)(2,1)S(1)}, bf16[1,128,1536]{2,1,0:T(8,128)(2,1)}, u32[]{:S(2)}) copy-start(bf16[1,128,1536]{2,1,0:T(8,128)(2,1)} %param.19) | copy-start | bytes 1179652
  (19 other events, 95.5 us)
Sparse Core Ops, SparseCore 0:
  12.9 97.4 all-gather.2
  114.3 91.4 all-gather.4
  259.8 178.4 reduce-scatter.1
  444.2 141.5 all-reduce.4
  588.6 25.2 all-reduce.2
where the time goes:
time: 624 us; the launch traced here: 622 us
  waiting for transfers between devices  361 us (58%)
  blocking collectives  73.4 us (12%)
  local copies, waits for them, and re-layouts  64.7 us (10%)
  matrix products  57.6 us (9%)
  other arithmetic  39.9 us (6%)
  between operations  14.5 us (2%)
  starting transfers between devices  10.4 us (2%)
    psum x1, waiting for transfers between devices, on_device(): lax.psum((local_kernel, local_gain), ('seq', 'utt'))  146 us
    all_gather x1, waiting for transfers between devices, on_device(): lax.all_gather(keys, 'seq', axis=0, tiled=True)  89.4 us
    psum x1, blocking collectives, on_device(): lax.psum((local_kernel, local_gain), ('seq', 'utt'))  73.4 us
    reduce_scatter x1, waiting for transfers between devices, on_device(): lax.psum_scatter(lax.dot_general(act, grad_now, (((0,), (0,)), ((), ())),...  49.7 us
    all_gather x1, waiting for transfers between devices, on_device(): lax.all_gather(values, 'seq', axis=0, tiled=True)  48.4 us
    psum x1, waiting for transfers between devices, on_device(): lax.psum(shares.astype(jnp.bfloat16), 'utt').astype(jnp.float32)  26.5 us
    another operation x33, local copies, waits for them, and re-layouts, on_device(): jnp.stack([jnp.sum(dz * taps_f[tap:tap + count], axis=0) for tap in range...  25.1 us
    dot_general x1, matrix products, attend_piece(): jnp.einsum('htf,fhd->thd', expo.astype(jnp.bfloat16), value_heads, prefer...  17 us
  transfers between devices with their start and end apart: 9, of which 6 were waited for; matrix products, arithmetic and copies ran while one was open for 18% of the time, Pallas kernels for 0%

commit v1 on v0

--- a/solution.py
+++ b/solution.py
@@ -3,12 +3,229 @@
 import jax
 import jax.numpy as jnp
 from jax import lax
+from jax.experimental import pallas as pl
+from jax.experimental.pallas import tpu as pltpu
 from jax.sharding import PartitionSpec as P
 
 D = 1536
 HEADS = 8
 HEAD_DIM = 96
+WIDE = HEADS * HEAD_DIM
 KER = 32
+BLOCK = 128
+HALF = 512
+LOG2E = 1.4426950408889634
+
+OWN, SIB, ZM, ZP, Z2, SIB_ZM, SIB_ZP, SIB_Z2 = range(8)
+
+
+def rows_norm(values):
+    mean = jnp.mean(values, axis=-1, keepdims=True)
+    centered = values - mean
+    rstd = lax.rsqrt(jnp.mean(centered * centered, axis=-1, keepdims=True) + 1e-05)
+    return centered * rstd, rstd
+
+
+def matmul(a, b, da=1, db=0):
+    return lax.dot_general(a, b, (((da,), (db,)), ((), ())), preferred_element_type=jnp.float32)
+
+
+def attention_kernel(
+    x_ref, gain_ref, wk_hbm, wv_hbm, wq_hbm, wo_hbm,
+    hidden_ref,
+    wk, wv, wq, wo, normed, kv_out, q_out, kv, qt, acc, top, mix_out, mixt,
+    wsem, kv_send, kv_recv, q_send, q_recv, m_send, m_recv, r_send, r_recv, lsem,
+):
+    s = lax.axis_index("seq")
+    z = s // 16
+    h = (s % 16) // 2
+    c = s % 2
+
+    def dev(zz, hh, cc):
+        return {"seq": zz * 16 + hh * 2 + cc}
+
+    peers = [dev(z, (h + k) % 8, c) for k in range(1, 8)]
+    up, down = dev((z + 1) % 4, h, c), dev((z + 3) % 4, h, c)
+    sibling = dev(z, h, 1 - c)
+
+    def remote(src, dst, send, recv, to):
+        copy = pltpu.make_async_remote_copy(
+            src_ref=src, dst_ref=dst, send_sem=send, recv_sem=recv,
+            device_id=to, device_id_type=pl.DeviceIdType.MESH,
+        )
+        copy.start()
+        return copy
+
+    loads = [
+        pltpu.make_async_copy(src, dst, wsem.at[i])
+        for i, (src, dst) in enumerate(((wk_hbm, wk), (wv_hbm, wv), (wq_hbm, wq), (wo_hbm, wo)))
+    ]
+    for load in loads:
+        load.start()
+    for slot in range(16):
+        kv[slot, 192:208, :] = jnp.ones((16, HALF), jnp.bfloat16)
+
+    barrier = pltpu.get_barrier_semaphore()
+    for to in peers + [up, down, sibling]:
+        pl.semaphore_signal(barrier, inc=1, device_id=to, device_id_type=pl.DeviceIdType.MESH)
+
+    xhat, unused_item = rows_norm(x_ref[...].astype(jnp.float32))
+    normed[...] = (xhat * gain_ref[...]).astype(jnp.bfloat16)
+    loads[0].wait()
+    k_rows = matmul(normed[...], wk[...]).T.astype(jnp.bfloat16)
+    for i in range(HEADS):
+        kv_out[i, 0:96, :] = k_rows[i * 96 : i * 96 + 96, :]
+    loads[1].wait()
+    v_rows = matmul(normed[...], wv[...]).T.astype(jnp.bfloat16)
+    for i in range(HEADS):
+        kv_out[i, 96:192, :] = v_rows[i * 96 : i * 96 + 96, :]
+
+    pl.semaphore_wait(barrier, 10)
+    mine = pl.ds(pl.multiple_of((h % 4) * 128, 128), 128)
+    kv_copies = [
+        remote(kv_out.at[(h + k) % 8], kv.at[h // 4, 0:192, mine],
+               kv_send.at[k - 1], kv_recv.at[k - 1], peers[k - 1])
+        for k in range(1, 8)
+    ]
+    kv_self = pltpu.make_async_copy(kv_out.at[h], kv.at[h // 4, 0:192, mine], lsem.at[0])
+    kv_self.start()
+
+    loads[2].wait()
+    scale = LOG2E / math.sqrt(HEAD_DIM)
+    q_rows = (matmul(normed[...], wq[...]) * scale).T.astype(jnp.bfloat16)
+    for i in range(HEADS):
+        q_out[i] = q_rows[i * 96 : i * 96 + 96, :]
+    lanes = pl.ds(pl.multiple_of(h * 128, 128), 128)
+    q_copies = [
+        remote(q_out.at[(h + k) % 8], qt.at[:, lanes],
+               q_send.at[k - 1], q_recv.at[k - 1], peers[k - 1])
+        for k in range(1, 8)
+    ]
+    q_self = pltpu.make_async_copy(q_out.at[h], qt.at[:, lanes], lsem.at[1])
+    q_self.start()
+
+    sent = []
+
+    def forward(slot, half, to, to_slot):
+        sem = len(sent)
+        copy = remote(kv.at[2 * slot + half, 0:192], kv.at[2 * to_slot + half, 0:192],
+                      r_send.at[sem], r_recv.at[sem], to)
+        sent.append(copy)
+        return copy
+
+    acc[...] = jnp.zeros_like(acc)
+    top[...] = jnp.full_like(top, -1e30)
+
+    def attend(*halves):
+        halves = [2 * slot + half for slot, half in halves]
+        scores = [matmul(kv[i, 0:96, :], qt[...], 0, 0) for i in halves]
+        before = top[0:1, :]
+        newest = before
+        for part in scores:
+            newest = jnp.maximum(newest, jnp.max(part, axis=0, keepdims=True))
+        total = acc[...] * jnp.exp2(before - newest)
+        for i, part in zip(halves, scores):
+            total += matmul(kv[i, 96:208, :], jnp.exp2(part - newest).astype(jnp.bfloat16))
+        acc[...] = total
+        top[0:1, :] = newest
+
+    for copy in kv_copies:
+        copy.wait_recv()
+    kv_self.wait()
+    zm0 = forward(OWN, 0, up, ZM)
+    zp1 = forward(OWN, 1, down, ZP)
+    sib0 = forward(OWN, 0, sibling, SIB)
+    sib1 = forward(OWN, 1, sibling, SIB)
+    zm1 = forward(OWN, 1, up, ZM)
+    zp0 = forward(OWN, 0, down, ZP)
+    for copy in q_copies:
+        copy.wait_recv()
+    q_self.wait()
+    attend((OWN, 0), (OWN, 1))
+    zm0.wait_recv()
+    z20 = forward(ZM, 0, up, Z2)
+    szm0 = forward(ZM, 0, sibling, SIB_ZM)
+    zp1.wait_recv()
+    z21 = forward(ZP, 1, down, Z2)
+    szp1 = forward(ZP, 1, sibling, SIB_ZP)
+    sib0.wait_recv()
+    sib1.wait_recv()
+    attend((SIB, 0), (SIB, 1), (ZM, 0), (ZP, 1))
+    zm1.wait_recv()
+    szm1 = forward(ZM, 1, sibling, SIB_ZM)
+    zp0.wait_recv()
+    szp0 = forward(ZP, 0, sibling, SIB_ZP)
+    szm0.wait_recv()
+    szp1.wait_recv()
+    attend((SIB_ZM, 0), (SIB_ZP, 1), (ZM, 1), (ZP, 0))
+    z20.wait_recv()
+    sz20 = forward(Z2, 0, sibling, SIB_Z2)
+    z21.wait_recv()
+    sz21 = forward(Z2, 1, sibling, SIB_Z2)
+    szm1.wait_recv()
+    szp0.wait_recv()
+    attend((SIB_ZM, 1), (SIB_ZP, 0), (Z2, 0), (Z2, 1))
+    sz20.wait_recv()
+    sz21.wait_recv()
+    attend((SIB_Z2, 0), (SIB_Z2, 1))
+
+    mix_out[...] = (acc[0:96, :] / acc[96:97, :]).astype(jnp.bfloat16)
+    band = pl.ds(pl.multiple_of(h * 96, 96), 96)
+    m_copies = []
+    for k in range(1, 8):
+        to_lanes = pl.ds(pl.multiple_of(((h + k) % 8) * 128, 128), 128)
+        m_copies.append(
+            remote(mix_out.at[:, to_lanes], mixt.at[band, :],
+                   m_send.at[k - 1], m_recv.at[k - 1], peers[k - 1])
+        )
+    m_self = pltpu.make_async_copy(mix_out.at[:, lanes], mixt.at[band, :], lsem.at[2])
+    m_self.start()
+    loads[3].wait()
+    for copy in m_copies:
+        copy.wait_recv()
+    m_self.wait()
+    hidden_ref[...] = (x_ref[...].astype(jnp.float32) + matmul(mixt[...], wo[...], 0, 0)).astype(
+        jnp.bfloat16
+    )
+    for copy in kv_copies + q_copies + sent + m_copies:
+        copy.wait_send()
+
+
+def attention(x, gain, w_key, w_value, w_query, w_out):
+    bf = jnp.bfloat16
+    vmem = pl.BlockSpec(memory_space=pltpu.VMEM)
+    hbm = pl.BlockSpec(memory_space=pl.ANY)
+    dma = pltpu.SemaphoreType.DMA
+    return pl.pallas_call(
+        attention_kernel,
+        name="attention",
+        out_shape=jax.ShapeDtypeStruct((BLOCK, D), bf),
+        in_specs=[vmem, vmem, hbm, hbm, hbm, hbm],
+        out_specs=vmem,
+        scratch_shapes=[
+            pltpu.VMEM((D, WIDE), bf),
+            pltpu.VMEM((D, WIDE), bf),
+            pltpu.VMEM((D, WIDE), bf),
+            pltpu.VMEM((WIDE, D), bf),
+            pltpu.VMEM((BLOCK, D), bf),
+            pltpu.VMEM((HEADS, 192, 128), bf),
+            pltpu.VMEM((HEADS, 96, 128), bf),
+            pltpu.VMEM((16, 208, HALF), bf),
+            pltpu.VMEM((96, 1024), bf),
+            pltpu.VMEM((112, 1024), jnp.float32),
+            pltpu.VMEM((8, 1024), jnp.float32),
+            pltpu.VMEM((96, 1024), bf),
+            pltpu.VMEM((WIDE, 128), bf),
+            dma((4,)), dma((7,)), dma((7,)), dma((7,)), dma((7,)), dma((7,)), dma((7,)),
+            dma((14,)), dma((14,)), dma((3,)),
+        ],
+        compiler_params=pltpu.CompilerParams(
+            collective_id=0, has_side_effects=True, vmem_limit_bytes=48 << 20
+        ),
+        cost_estimate=pl.CostEstimate(
+            flops=6 * 10**9, bytes_accessed=10 * 2**20, transcendentals=2**23
+        ),
+    )(x, gain, w_key, w_value, w_query, w_out)
 
 
 def with_halo(block, sides, width):
@@ -29,24 +246,6 @@
     centered = values - mean
     rstd = lax.rsqrt(jnp.mean(centered * centered, axis=-1, keepdims=True) + 1e-05)
     return (centered * rstd, rstd)
-
-
-def attend_piece(carry, key_rows, value_rows, query_heads):
-    running, total, accum = carry
-    count = key_rows.shape[0]
-    key_heads = key_rows.reshape(count, HEADS, HEAD_DIM)
-    value_heads = value_rows.reshape(count, HEADS, HEAD_DIM)
-    scores = jnp.einsum("thd,fhd->htf", query_heads, key_heads, preferred_element_type=jnp.float32)
-    scores = scores * (1.0 / math.sqrt(HEAD_DIM))
-    newest = jnp.maximum(running, jnp.max(scores, axis=-1))
-    factor = jnp.exp(running - newest)
-    expo = jnp.exp(scores - newest[:, :, None])
-    total = jnp.sum(expo, axis=-1)
-    summed = jnp.einsum(
-        "htf,fhd->thd", expo.astype(jnp.bfloat16), value_heads, preferred_element_type=jnp.float32
-    )
-    accum = accum * factor.T[:, :, None] + summed
-    return (newest, total, accum)
 
 
 def depthwise(source, kernel, count):
@@ -73,38 +272,12 @@
     w_point,
     cotangent,
 ):
-    input_rows = inputs[0].astype(jnp.float32)
-    count = input_rows.shape[0]
+    count = inputs.shape[1]
     width = D
     half = KER // 2
-    standardized_input, unused_item = standardize_rows(input_rows)
-    normed_rows = (standardized_input * attention_norm_gain).astype(jnp.bfloat16)
-    query_heads = (
-        jnp.dot(normed_rows, w_query, preferred_element_type=jnp.float32)
-        .astype(jnp.bfloat16)
-        .reshape(count, HEADS, HEAD_DIM)
-    )
-    start_carry = (
-        jnp.full((HEADS, count), -1e30, jnp.float32),
-        jnp.zeros((HEADS, count), jnp.float32),
-        jnp.zeros((count, HEADS, HEAD_DIM), jnp.float32),
-    )
-    keys = jnp.dot(normed_rows, w_key, preferred_element_type=jnp.float32).astype(jnp.bfloat16)
-    values = jnp.dot(normed_rows, w_value, preferred_element_type=jnp.float32).astype(jnp.bfloat16)
-    carry = attend_piece(
-        start_carry,
-        lax.all_gather(keys, "seq", axis=0, tiled=True),
-        lax.all_gather(values, "seq", axis=0, tiled=True),
-        query_heads,
-    )
-    mixed = (
-        (carry[2] / carry[1].T[:, :, None]).reshape(count, HEADS * HEAD_DIM).astype(jnp.bfloat16)
-    )
-    hidden_f = (
-        (input_rows + jnp.dot(mixed, w_out, preferred_element_type=jnp.float32))
-        .astype(jnp.bfloat16)
-        .astype(jnp.float32)
-    )
+    hidden_f = attention(
+        inputs[0], attention_norm_gain[None], w_key, w_value, w_query, w_out
+    ).astype(jnp.float32)
     hhat, rstd = standardize_rows(hidden_f)
     conv_in = (hhat * gain_conv).astype(jnp.bfloat16)
     grad_now = cotangent[0]

time: 624 us -> 289 us (0.46)
  waiting for transfers between devices: 361 us -> 109 us
  local copies, waits for them, and re-layouts: 64.7 us -> 8.57 us
  matrix products: 57.6 us -> 12.6 us
  Pallas kernels: 0 us -> 42.5 us
  other arithmetic: 39.9 us -> 17.8 us
    psum x1, waiting for transfers between devices: 146 us -> 0.03 us  [on_device(): lax.psum((local_kernel, local_gain), ('seq', 'utt'))]
    all_gather x2 -> x0, waiting for transfers between devices: 138 us -> none  [the longest x1 89.4 us: on_device(): lax.all_gather(keys, 'seq', axis=0, tiled=True)]
    pallas_call x0 -> x1, Pallas kernels: none -> 42.5 us  [attention(): pl.pallas_call(attention_kernel, name='attention', out_shape=jax.ShapeDty...]
    dot_general x6 -> x0, matrix products: 42.1 us -> none  [the longest x1 17 us: attend_piece(): jnp.einsum('htf,fhd->thd', expo.astype(jnp.bfloat16), value_heads, prefer...]
    all_gather x2 -> x0, local copies, waits for them, and re-layouts: 33.3 us -> none  [the longest x1 16.6 us: on_device(): lax.all_gather(values, 'seq', axis=0, tiled=True)]
    reduce_scatter x1, waiting for transfers between devices: 49.7 us -> 81.9 us  [on_device(): lax.psum_scatter(lax.dot_general(act, grad_now, (((0,), (0,)), ((), ())),...]
    another operation x33, local copies, waits for them, and re-layouts: 25.1 us -> 2.97 us  [on_device(): jnp.stack([jnp.sum(dz * taps_f[tap:tap + count], axis=0) for tap in range...]
    reduce_sum x1 -> x0, other arithmetic: 14.2 us -> none  [attend_piece(): total = jnp.sum(expo, axis=-1)]
  transfers between devices with their start and end apart: 9 -> 7, of which waited for: 6 -> 3; matrix products, arithmetic and copies ran while one was open for 18% -> 8% of each run, Pallas kernels for 0% -> 0%
where the time goes in v1:
time: 289 us
  waiting for transfers between devices  109 us (38%)
  blocking collectives  71.4 us (25%)
  Pallas kernels  42.5 us (15%)
  other arithmetic  17.8 us (6%)
  between operations  15.9 us (6%)
  matrix products  12.6 us (4%)
  starting transfers between devices  11 us (4%)
  local copies, waits for them, and re-layouts  8.57 us (3%)
    reduce_scatter x1, waiting for transfers between devices, on_device(): lax.psum_scatter(lax.dot_general(act, grad_now, (((0,), (0,)), ((), ())),...  81.9 us
    psum x1, blocking collectives, on_device(): lax.psum((local_kernel, local_gain), ('seq', 'utt'))  71.4 us
    pallas_call x1, Pallas kernels, attention(): pl.pallas_call(attention_kernel, name='attention', out_shape=jax.ShapeDty...  42.5 us
    psum x1, waiting for transfers between devices, on_device(): lax.psum(shares.astype(jnp.bfloat16), 'utt').astype(jnp.float32)  24.2 us
    ppermute x2, starting transfers between devices, with_halo(): lax.ppermute(lax.slice_in_dim(block, block.shape[dim] - width, None, axis...  6.57 us
    dot_general x1, matrix products, on_device(): lax.dot_general(grad_now, w_point, (((1,), (1,)), ((), ())), preferred_el...  5.87 us
  transfers between devices with their start and end apart: 7, of which 3 were waited for; matrix products, arithmetic and copies ran while one was open for 8% of the time, Pallas kernels for 0%

profile of v1, /device:TPU:1, one launch (start us, length us, event | category | flops | bytes accessed | tf_op | source)
XLA Modules:
  0.0 289.0 jit_solution(16643979433407347896)
XLA Ops:
  8.0 0.7 broadcast_in_dim.6.gain_ref
  8.7 1.7 copy-done
  10.4 1.7 copy-done.1
  12.1 1.0 copy-done.2
  13.1 42.5 %attention.1 = bf16[128,1536]{1,0:T(8,128)(2,1)S(1)} custom-call(bf16[128,1536]{1,0:T(8,128)(2,1)S(1)} %bitcast.15, f32[1,1536]{1,0:T(1,128)S(1)} %broadcast_in_dim.6.gain_ref, bf16[1536,768]{1,0:T(8,128)(2,1)S(1)} %copy-done, bf16[1536,768]{1,0:T(8,128)(2,1)S(1)} %copy-done.1, bf16[1536,768]{1,0:T(8,128)(2,1)} %wq_hbm.1, bf16[768,1536]{1,0:T(8,128)(2,1)} %wo_hbm.1), custom_call_target="tpu_custom_call" | custom-call | flops 6000000000 | bytes 10485760 | tf_op jit(solution)/shard_map/attention/pallas_call | solution.py:199
  55.6 0.1 convert_reduce_fusion
  55.7 0.3 fusion.15
  56.0 0.3 fusion.8
  56.3 4.7 %collective-permute-start = (bf16[16,1536]{1,0:T(8,128)(2,1)S(1)}, bf16[16,1536]{1,0:T(8,128)(2,1)S(1)}, u32[]{:S(2)}, u32[]{:S(2)}) collective-permute-start(bf16[16,1536]{1,0:T(8,128)(2,1)S(1)} %get-tuple-element.76), channel_id=1, source_target_pairs={{0,2},{2,4},{4,6},{6,8},{8,10},{10,12},{12,14},{14,16},{16,18},{18... | collective-permute-start | bytes 147464 | tf_op jit(solution)/shard_map/ppermute | solution.py:236
  61.0 1.9 collective-permute-start.1
  62.9 0.3 slice_reduce_fusion.31
  63.2 0.2 slice_reduce_fusion.30
  63.5 2.9 %collective-permute-done.1 = bf16[16,1536]{1,0:T(8,128)(2,1)S(1)} collective-permute-done((bf16[16,1536]{1,0:T(8,128)(2,1)S(1)}, bf16[16,1536]{1,0:T(8,128)(2,1)S(1)}, u32[]{:S(2)}, u32[]{:S(2)}) %collective-permute-start.1) | collective-permute-done | bytes 49184 | tf_op jit(solution)/shard_map/ppermute | solution.py:239
  66.4 3.7 %multiply_add_fusion = f32[128,1536]{1,0:T(8,128)S(1)} fusion(bf16[128,1536]{1,0:T(8,128)(2,1)S(1)} %fusion.8, bf16[16,1536]{1,0:T(8,128)(2,1)S(1)} %collective-permute-done.1, bf16[16,1536]{1,0:T(8,128)(2,1)S(1)} %collective-permute-done, f32[1536]{0:T(1024)S(1)} %get-tuple-element.70, f32[1536]{0:T(1024)S(1)} %get-tuple-element.71, ...), kind=kLoop, calls=%fused_computation.178 | loop fusion | flops 36962304 | bytes 1474560 | tf_op jit(solution)/shard_map/add | solution.py:254
  70.1 5.1 %fusion.109 = f32[1536,1536]{1,0:T(8,128)} fusion(bf16[1,128,1536]{2,1,0:T(8,128)(2,1)S(1)} %copy-done.3, f32[128,1536]{1,0:T(8,128)S(1)} %multiply_add_fusion), kind=kOutput, calls=%fused_computation.235 | convolution fusion | flops 604962816 | bytes 10616832 | tf_op jit(solution)/shard_map/dot_general | solution.py:313
  75.3 0.1 maximum_convert_fusion.1
  75.4 5.9 %fusion.16 = (f32[1536]{0:T(1024)S(1)}, f32[1536]{0:T(1024)S(1)}, f32[1536]{0:T(1024)S(1)}, f32[1536]{0:T(1024)S(1)}, f32[1536]{0:T(1024)S(1)}, /*index=5*/f32[1...) fusion(f32[160,1536]{1,0:T(8,128)S(1)} %maximum_convert_fusion., ...), kind=kOutput, calls=%fused_computation.50 | convolution fusion | flops 612799488 | bytes 21344256 | tf_op jit(solution)/shard_map/dot_general | solution.py:286
  81.3 1.9 collective-permute-start.2
  83.2 2.4 collective-permute-start.3
  85.6 1.5 fusion.34
  87.2 1.6 fusion.1
  89.3 2.8 stack.131
  92.1 0.1 maximum_convert_fusion
  92.2 5.2 %fusion.14 = (f32[1536]{0:T(1024)S(1)}, f32[128]{0:T(128)S(1)}, f32[128]{0:T(128)S(1)}, f32[128,1536]{1,0:T(8,128)S(1)}) fusion(bf16[128,1536]{1,0:T(8,128)(2,1)S(1)} %attention.1, f32[128]{0:T(128)S(1)} %add_rsqrt_fusion, f32[128]{0:T(128)S(1)} %broadcast_multiply_fusion.4, f32[1536]{0:T(1024)S(1)} %copy-done.5, f32[160,1536]{1,0:T(8,128)S(1)} %maximum_convert_fusion, ...), kind=kLoop, calls=%fused_computation.47 | loop fusion | flops 14153984 | bytes 26556416 | tf_op jit(solution)/shard_map/reduce_sum | solution.py:302
  97.5 71.4 %psum.23 = f32[1536]{0:T(1024)S(1)} all-reduce(f32[1536]{0:T(1024)S(1)} %get-tuple-element.37), channel_id=1, replica_groups=mesh['seq'=64,'utt'=2] {'seq','utt'}, use_global_device_ids=true, to_apply=%region_40.0 | all-reduce | flops 1536 | bytes 12288 | tf_op jit(solution)/shard_map/psum | solution.py:311
  168.9 1.1 fusion.79
  170.0 0.6 broadcast_multiply_fusion.1
  170.6 81.9 %reduce-scatter.2.cloned.1.call-done = f32[24,1536]{1,0:T(8,128)} async-done(((f32[1536,1536]{1,0:T(8,128)}), f32[24,1536]{1,0:T(8,128)}) %reduce-scatter.2.cloned.1.call-update) | async-done | bytes 147472 | tf_op jit(solution)/shard_map/reduce_scatter | solution.py:312
  252.5 1.6 convert_element_type.169
  254.2 1.6 broadcast_multiply_fusion
  255.8 24.2 %all-reduce.3.cloned.1.call-done = bf16[24,1536]{1,0:T(8,128)(2,1)} async-done(((bf16[24,1536]{1,0:T(8,128)(2,1)}), bf16[24,1536]{1,0:T(8,128)(2,1)}) %all-reduce.3.cloned.1.call-update) | async-done | bytes 73744 | tf_op jit(solution)/shard_map/psum | solution.py:320
  280.0 1.6 convert_multiply_fusion
  (61 shorter events, 0.5 us)
Async XLA Ops:
  8.0 244.5 %reduce-scatter.2.cloned.1.call-start = ((), (), s32[]{:S(2)}) async-start(), calls=%async_computation.1 | async-start | bytes 9584640 | tf_op jit(solution)/shard_map/reduce_scatter | solution.py:312
  8.7 1.7 copy-start
  10.4 1.7 copy-start.1
  12.1 1.0 copy-start.2
  13.1 42.9 %copy-start.5 = (f32[1536]{0:T(1024)S(1)}, f32[1536]{0:T(1024)}, u32[]{:S(2)}) copy-start(f32[1536]{0:T(1024)} %param.16) | copy-start | bytes 18436
  13.1 49.8 %copy-start.4 = (f32[32,1536]{1,0:T(8,128)S(1)}, f32[32,1536]{1,0:T(8,128)}, u32[]{:S(2)}) copy-start(f32[32,1536]{1,0:T(8,128)} %param.17) | copy-start | bytes 589828
  13.1 57.0 %copy-start.3 = (bf16[1,128,1536]{2,1,0:T(8,128)(2,1)S(1)}, bf16[1,128,1536]{2,1,0:T(8,128)(2,1)}, u32[]{:S(2)}) copy-start(bf16[1,128,1536]{2,1,0:T(8,128)(2,1)} %param.19) | copy-start | bytes 1179652
  56.3 7.1 %collective-permute-start = (bf16[16,1536]{1,0:T(8,128)(2,1)S(1)}, bf16[16,1536]{1,0:T(8,128)(2,1)S(1)}, u32[]{:S(2)}, u32[]{:S(2)}) collective-permute-start(bf16[16,1536]{1,0:T(8,128)(2,1)S(1)} %get-tuple-element.76), channel_id=1, source_target_pairs={{0,2},{2,4},{4,6},{6,8},{8,10},{10,12},{12,14},{14,16},{16,18},{18... | collective-permute-start | bytes 147464 | tf_op jit(solution)/shard_map/ppermute | solution.py:236
  61.0 5.4 %collective-permute-start.1 = (bf16[16,1536]{1,0:T(8,128)(2,1)S(1)}, bf16[16,1536]{1,0:T(8,128)(2,1)S(1)}, u32[]{:S(2)}, u32[]{:S(2)}) collective-permute-start(bf16[16,1536]{1,0:T(8,128)(2,1)S(1)} %get-tuple-element.77), channel_id=1, source_target_pairs={{2,0},{4,2},{6,4},{8,6},{10,8},{12,10},{14,12},{16,14},{18,16},{20... | collective-permute-start | bytes 147464 | tf_op jit(solution)/shard_map/ppermute | solution.py:239
  75.2 179.0 %all-reduce.5.cloned.1.call-start = ((), (), s32[]{:S(2)}) async-start(), calls=%async_computation.3 | async-start | bytes 393216 | tf_op jit(solution)/shard_map/psum | solution.py:311
  75.2 11.9 %slice-start = ((s8[4718592]{0:T(1024)(128)(4,1)}), s8[4194304]{0:T(1024)(128)(4,1)S(1)}, s32[]{:S(2)}) async-start(s8[4718592]{0:T(1024)(128)(4,1)} %bitcast.16), calls=%async_computation.4 | async-start | bytes 8388608
  75.4 11.8 %slice-start.1 = ((s8[4718592]{0:T(1024)(128)(4,1)}), s8[524288]{0:T(1024)(128)(4,1)S(1)}, s32[]{:S(2)}) async-start(s8[4718592]{0:T(1024)(128)(4,1)} %bitcast.16), calls=%async_computation.5 | async-start | bytes 1048576
  81.3 10.9 %collective-permute-start.2 = (bf16[16,1536]{1,0:T(8,128)(2,1)S(1)}, bf16[16,1536]{1,0:T(8,128)(2,1)S(1)}, u32[]{:S(2)}, u32[]{:S(2)}) collective-permute-start(bf16[16,1536]{1,0:T(8,128)(2,1)S(1)} %get-tuple-element.74), channel_id=1, source_target_pairs={{0,2},{2,4},{4,6},{6,8},{8,10},{10,12},{12,14},{14,16},{16,18},{18... | collective-permute-start | bytes 147464 | tf_op jit(solution)/shard_map/ppermute | solution.py:236
  83.2 8.9 %collective-permute-start.3 = (bf16[16,1536]{1,0:T(8,128)(2,1)S(1)}, bf16[16,1536]{1,0:T(8,128)(2,1)S(1)}, u32[]{:S(2)}, u32[]{:S(2)}) collective-permute-start(bf16[16,1536]{1,0:T(8,128)(2,1)S(1)} %get-tuple-element.75), channel_id=1, source_target_pairs={{2,0},{4,2},{6,4},{8,6},{10,8},{12,10},{14,12},{16,14},{18,16},{20... | collective-permute-start | bytes 147464 | tf_op jit(solution)/shard_map/ppermute | solution.py:239
  92.1 187.9 %all-reduce.3.cloned.1.call-start = ((), (), s32[]{:S(2)}) async-start(), calls=%async_computation.2 | async-start | bytes 147456 | tf_op jit(solution)/shard_map/psum | solution.py:320
Sparse Core Ops, SparseCore 0:
  75.3 177.1 reduce-scatter.1
Sparse Core Ops, SparseCore 1:
  92.2 151.0 all-reduce.4
  254.2 25.7 all-reduce.2

commit v2 on v1

--- a/solution.py
+++ b/solution.py
@@ -31,10 +31,10 @@
 
 
 def attention_kernel(
-    x_ref, gain_ref, wk_hbm, wv_hbm, wq_hbm, wo_hbm,
-    hidden_ref,
+    x_ref, gain_ref, wk_hbm, wv_hbm, wq_hbm, wo_hbm, cot_hbm,
+    hidden_ref, cots_hbm,
     wk, wv, wq, wo, normed, kv_out, q_out, kv, qt, acc, top, mix_out, mixt,
-    wsem, kv_send, kv_recv, q_send, q_recv, m_send, m_recv, r_send, r_recv, lsem,
+    wsem, kv_send, kv_recv, q_send, q_recv, m_send, m_recv, r_send, r_recv, c_send, c_recv, lsem,
 ):
     s = lax.axis_index("seq")
     z = s // 16
@@ -138,6 +138,18 @@
     sib1 = forward(OWN, 1, sibling, SIB)
     zm1 = forward(OWN, 1, up, ZM)
     zp0 = forward(OWN, 0, down, ZP)
+    x, side = h % 4, h // 4
+    own_rows = pl.ds(pl.multiple_of((x * 2 + c) * BLOCK, BLOCK), BLOCK)
+    c_self = pltpu.make_async_copy(cot_hbm, cots_hbm.at[own_rows], lsem.at[3])
+    c_self.start()
+    c_copies = [
+        remote(cot_hbm, cots_hbm.at[own_rows], c_send.at[k - 1], c_recv.at[k - 1],
+               dev(z, side * 4 + (x + k) % 4, c))
+        for k in range(1, 4)
+    ]
+    c_copies.append(
+        remote(cot_hbm, cots_hbm.at[own_rows], c_send.at[3], c_recv.at[3], sibling)
+    )
     for copy in q_copies:
         copy.wait_recv()
     q_self.wait()
@@ -164,6 +176,12 @@
     sz21 = forward(Z2, 1, sibling, SIB_Z2)
     szm1.wait_recv()
     szp0.wait_recv()
+    for k in range(1, 4):
+        c_copies[k - 1].wait_recv()
+        rows = pl.ds(pl.multiple_of(((x + 4 - k) % 4 * 2 + c) * BLOCK, BLOCK), BLOCK)
+        c_copies.append(
+            remote(cots_hbm.at[rows], cots_hbm.at[rows], c_send.at[3 + k], c_recv.at[3 + k], sibling)
+        )
     attend((SIB_ZM, 1), (SIB_ZP, 0), (Z2, 0), (Z2, 1))
     sz20.wait_recv()
     sz21.wait_recv()
@@ -187,11 +205,14 @@
     hidden_ref[...] = (x_ref[...].astype(jnp.float32) + matmul(mixt[...], wo[...], 0, 0)).astype(
         jnp.bfloat16
     )
-    for copy in kv_copies + q_copies + sent + m_copies:
+    for copy in c_copies[3:]:
+        copy.wait_recv()
+    c_self.wait()
+    for copy in kv_copies + q_copies + sent + m_copies + c_copies:
         copy.wait_send()
 
 
-def attention(x, gain, w_key, w_value, w_query, w_out):
+def attention(x, gain, w_key, w_value, w_query, w_out, cot):
     bf = jnp.bfloat16
     vmem = pl.BlockSpec(memory_space=pltpu.VMEM)
     hbm = pl.BlockSpec(memory_space=pl.ANY)
@@ -199,9 +220,9 @@
     return pl.pallas_call(
         attention_kernel,
         name="attention",
-        out_shape=jax.ShapeDtypeStruct((BLOCK, D), bf),
-        in_specs=[vmem, vmem, hbm, hbm, hbm, hbm],
-        out_specs=vmem,
+        out_shape=(jax.ShapeDtypeStruct((BLOCK, D), bf), jax.ShapeDtypeStruct((8 * BLOCK, D), bf)),
+        in_specs=[vmem, vmem, hbm, hbm, hbm, hbm, hbm],
+        out_specs=(vmem, hbm),
         scratch_shapes=[
             pltpu.VMEM((D, WIDE), bf),
             pltpu.VMEM((D, WIDE), bf),
@@ -217,47 +238,266 @@
             pltpu.VMEM((96, 1024), bf),
             pltpu.VMEM((WIDE, 128), bf),
             dma((4,)), dma((7,)), dma((7,)), dma((7,)), dma((7,)), dma((7,)), dma((7,)),
-            dma((14,)), dma((14,)), dma((3,)),
+            dma((14,)), dma((14,)), dma((7,)), dma((7,)), dma((4,)),
         ],
         compiler_params=pltpu.CompilerParams(
-            collective_id=0, has_side_effects=True, vmem_limit_bytes=48 << 20
+            collective_id=0, has_side_effects=True, vmem_limit_bytes=60 << 20
         ),
         cost_estimate=pl.CostEstimate(
             flops=6 * 10**9, bytes_accessed=10 * 2**20, transcendentals=2**23
         ),
-    )(x, gain, w_key, w_value, w_query, w_out)
-
-
-def with_halo(block, sides, width):
-    for axis, dim in sides:
-        count = lax.axis_size(axis)
-        forward = [(i, i + 1) for i in range(count - 1)]
-        backward = [(target, source) for source, target in forward]
-        low = lax.ppermute(
-            lax.slice_in_dim(block, block.shape[dim] - width, None, axis=dim), axis, forward
+    )(x, gain, w_key, w_value, w_query, w_out, cot)
+
+
+def conv_kernel(
+    hidden_ref, gain_ref, taps_ref, wp_hbm, cot_ref, cots_hbm,
+    out_ref, gh_ref, gp_ref, gk_ref, gg_ref,
+    wp, cots, hhat, ci, back, dz, act, act_t, act_out, act_in, edge, far, tile_out, tile_in,
+    y_out, y_in, part, sums, b_in, c_in, d_in, total,
+    lsem, e_send, e_recv, a_send, a_recv, b_send, b_recv, c_send, c_recv, d_send, d_recv,
+    g_send, g_recv, t_send, t_recv, y_send, y_recv,
+):
+    f32, bf = jnp.float32, jnp.bfloat16
+    s = lax.axis_index("seq")
+    u = lax.axis_index("utt")
+    z, y_hi, x, c = s // 16, (s // 8) % 2, (s // 2) % 4, s % 2
+    p, y = s % 8, y_hi * 2 + u
+    right, left = {"seq": (s + 1) % 64}, {"seq": (s + 63) % 64}
+    group = [{"seq": s // 8 * 8 + (p + k) % 8} for k in range(1, 8)]
+    z_peers = [{"seq": (z + k) % 4 * 16 + s % 16} for k in range(1, 4)]
+    y_peers = [
+        {"seq": z * 16 + (y + k) % 4 // 2 * 8 + p, "utt": (y + k) % 4 % 2} for k in range(1, 4)
+    ]
+    copies = []
+
+    def remote(src, dst, send, recv, to):
+        copy = pltpu.make_async_remote_copy(
+            src_ref=src, dst_ref=dst, send_sem=send, recv_sem=recv,
+            device_id=to, device_id_type=pl.DeviceIdType.MESH,
         )
-        high = lax.ppermute(lax.slice_in_dim(block, 0, width, axis=dim), axis, backward)
-        block = jnp.concatenate([low, block, high], axis=dim)
-    return block
-
-
-def standardize_rows(values):
-    mean = jnp.mean(values, axis=-1, keepdims=True)
-    centered = values - mean
-    rstd = lax.rsqrt(jnp.mean(centered * centered, axis=-1, keepdims=True) + 1e-05)
-    return (centered * rstd, rstd)
-
-
-def depthwise(source, kernel, count):
-    result = jnp.zeros((count, source.shape[1]), jnp.float32)
-    for tap in range(kernel.shape[0]):
-        result = result + kernel[tap] * source[tap : tap + count].astype(jnp.float32)
-    return result
-
-
-def swish_grad(values):
-    sig = jax.nn.sigmoid(values)
-    return sig * (1.0 + values * (1.0 - sig))
+        copy.start()
+        copies.append(copy)
+        return copy
+
+    wp_load = pltpu.make_async_copy(wp_hbm, wp, lsem.at[0])
+    wp_load.start()
+    cots_load = pltpu.make_async_copy(cots_hbm, cots, lsem.at[1])
+    cots_load.start()
+    barrier = pltpu.get_barrier_semaphore()
+    for to in [right, left] + group + z_peers + y_peers:
+        pl.semaphore_signal(barrier, inc=1, device_id=to, device_id_type=pl.DeviceIdType.MESH)
+
+    normed, rstd = rows_norm(hidden_ref[...].astype(f32))
+    conv_in = (normed * gain_ref[...]).astype(bf)
+    edge[0] = conv_in[BLOCK - 16 :, :]
+    edge[1] = conv_in[:16, :]
+    pl.semaphore_wait(barrier, 15)
+    halo = [
+        remote(edge.at[0], far.at[0], e_send.at[0], e_recv.at[0], right),
+        remote(edge.at[1], far.at[1], e_send.at[1], e_recv.at[1], left),
+    ]
+    for l in range(12):
+        hhat[l] = normed[:, l * 128 : l * 128 + 128]
+        ci[l, 16:144, :] = conv_in[:, l * 128 : l * 128 + 128].astype(f32)
+    sums[480:512, :] = jnp.zeros((32, 128), f32)
+    wp_load.wait()
+    grads = matmul(cot_ref[...], wp[...], 1, 1)
+    for l in range(12):
+        back[l] = grads[:, l * 128 : l * 128 + 128]
+
+    def place_halo(ref, slot):
+        low = jnp.where(s > 0, far[slot].astype(f32), 0.0)
+        high = jnp.where(s < 63, far[slot + 1].astype(f32), 0.0)
+        for l in range(12):
+            ref[l, 0:16, :] = low[:, l * 128 : l * 128 + 128]
+            ref[l, 144:160, :] = high[:, l * 128 : l * 128 + 128]
+
+    for copy in halo:
+        copy.wait_recv()
+    place_halo(ci, 0)
+
+    def forward(l, carry):
+        conv = jnp.zeros((BLOCK, 128), f32)
+        for j in range(KER):
+            conv += taps_ref[l, j : j + 1, :] * ci[l, j : j + BLOCK, :]
+        sig = 1.0 / (1.0 + jnp.exp(-conv))
+        rounded = (conv * sig).astype(bf)
+        lanes = pl.ds(pl.multiple_of(l * 128, 128), 128)
+        act[:, lanes] = rounded
+        act_t[lanes, :] = rounded.astype(f32).T
+        grad = back[l] * (sig * (1.0 + conv * (1.0 - sig)))
+        dz[l, 16:144, :] = grad
+        for j0 in range(0, KER, 8):
+            rows = [
+                jnp.sum(grad * ci[l, j : j + BLOCK, :], axis=0, keepdims=True)
+                for j in range(j0, j0 + 8)
+            ]
+            sums[pl.ds(pl.multiple_of(l * 40 + j0, 8), 8), :] = jnp.concatenate(rows, axis=0)
+        return carry
+
+    lax.fori_loop(0, 12, forward, 0)
+    for l in range(12):
+        edge[2, :, l * 128 : l * 128 + 128] = dz[l, 128:144, :].astype(bf)
+        edge[3, :, l * 128 : l * 128 + 128] = dz[l, 16:32, :].astype(bf)
+    halo = [
+        remote(edge.at[2], far.at[2], e_send.at[2], e_recv.at[2], right),
+        remote(edge.at[3], far.at[3], e_send.at[3], e_recv.at[3], left),
+    ]
+    for i in range(8):
+        pieces = [act_t[24 * (8 * b + i) : 24 * (8 * b + i) + 24, :] for b in range(8)]
+        act_out[i] = jnp.concatenate(pieces, axis=0).astype(bf)
+    own_lanes = pl.ds(pl.multiple_of(p * 128, 128), 128)
+    act_copies = [
+        remote(act_out.at[(p + k) % 8], act_in.at[:, own_lanes],
+               a_send.at[k - 1], a_recv.at[k - 1], group[k - 1])
+        for k in range(1, 8)
+    ]
+    act_self = pltpu.make_async_copy(act_out.at[p], act_in.at[:, own_lanes], lsem.at[2])
+    act_self.start()
+    out_ref[...] = (hidden_ref[...].astype(f32) + matmul(act[...], wp[...])).astype(bf)
+
+    for copy in halo:
+        copy.wait_recv()
+    place_halo(dz, 2)
+    part[...] = jnp.zeros_like(part)
+
+    def backward(l, carry):
+        grad = jnp.zeros((BLOCK, 128), f32)
+        for j in range(KER):
+            grad += taps_ref[l, j : j + 1, :] * dz[l, 32 - j : 32 - j + BLOCK, :]
+        row = jnp.sum(grad * hhat[l], axis=0, keepdims=True)
+        sums[pl.ds(pl.multiple_of(l * 40 + 32, 8), 8), :] = jnp.concatenate(
+            [row, jnp.zeros((7, 128), f32)], axis=0
+        )
+        lanes = pl.ds(pl.multiple_of(l * 128, 128), 128)
+        g = grad * gain_ref[:, lanes]
+        back[l] = g
+        part[0] += g
+        part[1] += g * hhat[l]
+        return carry
+
+    lax.fori_loop(0, 12, backward, 0)
+    b_copies = [
+        remote(sums.at[pl.ds(pl.multiple_of((p + k) % 8 * 64, 64), 64)], b_in.at[k - 1],
+               b_send.at[k - 1], b_recv.at[k - 1], group[k - 1])
+        for k in range(1, 8)
+    ]
+
+    for copy in act_copies:
+        copy.wait_recv()
+    act_self.wait()
+    cots_load.wait()
+    tile = matmul(act_in[...], cots[...])
+    for b in range(4):
+        tile_out[b] = tile[48 * b : 48 * b + 48, :].astype(bf)
+    t_copies = [
+        remote(tile_out.at[(z + k) % 4], tile_in.at[k - 1],
+               t_send.at[k - 1], t_recv.at[k - 1], z_peers[k - 1])
+        for k in range(1, 4)
+    ]
+    for copy in b_copies:
+        copy.wait_recv()
+    own = pl.ds(pl.multiple_of(p * 64, 64), 64)
+    c_in[z] = sums[own, :] + sum(b_in[k] for k in range(7))
+    c_copies = [
+        remote(c_in.at[z], c_in.at[z], c_send.at[k], c_recv.at[k], z_peers[k]) for k in range(3)
+    ]
+
+    mean_g = jnp.sum(part[0], axis=-1, keepdims=True) * (1.0 / D)
+    mean_gh = jnp.sum(part[1], axis=-1, keepdims=True) * (1.0 / D)
+    for l in range(12):
+        lanes = slice(l * 128, l * 128 + 128)
+        inner = back[l] - mean_g - hhat[l] * mean_gh
+        gh_ref[:, lanes] = (cot_ref[:, lanes].astype(f32) + rstd * inner).astype(bf)
+
+    for copy in c_copies:
+        copy.wait_recv()
+    d_in[y] = c_in[0] + c_in[1] + c_in[2] + c_in[3]
+    d_copies = [
+        remote(d_in.at[y], d_in.at[y], d_send.at[k], d_recv.at[k], y_peers[k]) for k in range(3)
+    ]
+    for copy in t_copies:
+        copy.wait_recv()
+    mixed = tile_out[z].astype(f32) + sum(tile_in[k].astype(f32) for k in range(3))
+    for b in range(2):
+        y_out[b] = jnp.concatenate(
+            [mixed[24 * b : 24 * b + 24, : D // 2], mixed[24 * b : 24 * b + 24, D // 2 :]], axis=0
+        ).astype(bf)
+    yt_copies = [
+        remote(y_out.at[(y + k) % 4 // 2], y_in.at[y], y_send.at[k - 1], y_recv.at[k - 1],
+               y_peers[k - 1])
+        for k in range(1, 4)
+    ]
+    y_in[y] = y_out[y_hi]
+    for copy in d_copies:
+        copy.wait_recv()
+    total[own, :] = d_in[0] + d_in[1] + d_in[2] + d_in[3]
+    g_copies = [
+        remote(total.at[own], total.at[own], g_send.at[k], g_recv.at[k], group[k])
+        for k in range(7)
+    ]
+    scale = 1.0 / math.sqrt(2 * 64 * BLOCK)
+    for copy in yt_copies:
+        copy.wait_recv()
+    whole = sum(y_in[k].astype(f32) for k in range(4)) * scale
+    gp_ref[:, : D // 2] = whole[:24, :]
+    gp_ref[:, D // 2 :] = whole[24:, :]
+    for copy in g_copies:
+        copy.wait_recv()
+    for l in range(12):
+        lanes = slice(l * 128, l * 128 + 128)
+        gk_ref[:, lanes] = total[l * 40 : l * 40 + 32, :] * scale
+        gg_ref[:, lanes] = total[l * 40 + 32 : l * 40 + 33, :] * scale
+    for copy in copies:
+        copy.wait_send()
+
+
+def conv_module(hidden, gain, taps, w_point, cot, cots):
+    bf, f32 = jnp.bfloat16, jnp.float32
+    vmem = pl.BlockSpec(memory_space=pltpu.VMEM)
+    hbm = pl.BlockSpec(memory_space=pl.ANY)
+    dma = pltpu.SemaphoreType.DMA
+    shapes = [((BLOCK, D), bf), ((BLOCK, D), bf), ((24, D), f32), ((KER, D), f32), ((1, D), f32)]
+    return pl.pallas_call(
+        conv_kernel,
+        name="conv_module",
+        out_shape=tuple(jax.ShapeDtypeStruct(*shape) for shape in shapes),
+        in_specs=[vmem, vmem, vmem, hbm, vmem, hbm],
+        out_specs=(vmem,) * 5,
+        scratch_shapes=[
+            pltpu.VMEM((D, D), bf),
+            pltpu.VMEM((8 * BLOCK, D), bf),
+            pltpu.VMEM((12, BLOCK, 128), f32),
+            pltpu.VMEM((12, 160, 128), f32),
+            pltpu.VMEM((12, BLOCK, 128), f32),
+            pltpu.VMEM((12, 160, 128), f32),
+            pltpu.VMEM((BLOCK, D), bf),
+            pltpu.VMEM((D, BLOCK), f32),
+            pltpu.VMEM((8, 192, 128), bf),
+            pltpu.VMEM((192, 1024), bf),
+            pltpu.VMEM((4, 16, D), bf),
+            pltpu.VMEM((4, 16, D), bf),
+            pltpu.VMEM((4, 48, D), bf),
+            pltpu.VMEM((3, 48, D), bf),
+            pltpu.VMEM((2, 48, D // 2), bf),
+            pltpu.VMEM((4, 48, D // 2), bf),
+            pltpu.VMEM((2, BLOCK, 128), f32),
+            pltpu.VMEM((512, 128), f32),
+            pltpu.VMEM((7, 64, 128), f32),
+            pltpu.VMEM((4, 64, 128), f32),
+            pltpu.VMEM((4, 64, 128), f32),
+            pltpu.VMEM((512, 128), f32),
+            dma((3,)), dma((4,)), dma((4,)), dma((7,)), dma((7,)), dma((7,)), dma((7,)),
+            dma((3,)), dma((3,)), dma((3,)), dma((3,)), dma((7,)), dma((7,)),
+            dma((3,)), dma((3,)), dma((3,)), dma((3,)),
+        ],
+        compiler_params=pltpu.CompilerParams(
+            collective_id=1, has_side_effects=True, vmem_limit_bytes=60 << 20
+        ),
+        cost_estimate=pl.CostEstimate(
+            flops=3 * 10**9, bytes_accessed=10 * 2**20, transcendentals=2**18
+        ),
+    )(hidden, gain, taps, w_point, cot, cots)
 
 
 def on_device(
@@ -272,59 +512,14 @@
     w_point,
     cotangent,
 ):
-    count = inputs.shape[1]
-    width = D
-    half = KER // 2
-    hidden_f = attention(
-        inputs[0], attention_norm_gain[None], w_key, w_value, w_query, w_out
-    ).astype(jnp.float32)
-    hhat, rstd = standardize_rows(hidden_f)
-    conv_in = (hhat * gain_conv).astype(jnp.bfloat16)
-    grad_now = cotangent[0]
-    taps_source = with_halo(conv_in, (("seq", 0),), half)
-    conv = depthwise(taps_source, kernel, count)
-    back = lax.dot_general(
-        grad_now, w_point, (((1,), (1,)), ((), ())), preferred_element_type=jnp.float32
+    hidden, cots = attention(
+        inputs[0], attention_norm_gain[None], w_key, w_value, w_query, w_out, cotangent[0]
     )
-    dz = back * swish_grad(conv)
-    dz_pad = with_halo(dz.astype(jnp.bfloat16), (("seq", 0),), half).astype(dz.dtype)
-    act = (conv * jax.nn.sigmoid(conv)).astype(jnp.bfloat16)
-    layer_out = (hidden_f + jnp.dot(act, w_point, preferred_element_type=jnp.float32)).astype(
-        jnp.bfloat16
+    taps = kernel.reshape(KER, D // 128, 128).transpose(1, 0, 2)
+    layer_out, grad_hidden, grad_point, grad_kernel, grad_gain = conv_module(
+        hidden, gain_conv[None], taps, w_point, cotangent[0], cots
     )
-    taps_f = taps_source.astype(jnp.float32)
-    local_kernel = jnp.stack(
-        [jnp.sum(dz * taps_f[tap : tap + count], axis=0) for tap in range(KER)]
-    )
-    dconv_in = jnp.zeros((count, width), jnp.float32)
-    for tap in range(KER):
-        dconv_in = dconv_in + kernel[tap] * dz_pad[2 * half - tap : 2 * half - tap + count]
-    local_gain = jnp.sum(dconv_in * hhat, axis=0)
-    scaled = dconv_in * gain_conv
-    inner = (
-        scaled
-        - jnp.mean(scaled, axis=-1, keepdims=True)
-        - hhat * jnp.mean(scaled * hhat, axis=-1, keepdims=True)
-    )
-    grad_hidden = (grad_now.astype(jnp.float32) + rstd * inner).astype(jnp.bfloat16)
-    grad_scale = 1.0 / math.sqrt(lax.axis_size("utt") * lax.axis_size("seq") * count)
-    summed_kernel, summed_gain = lax.psum((local_kernel, local_gain), ("seq", "utt"))
-    shares = lax.psum_scatter(
-        lax.dot_general(
-            act, grad_now, (((0,), (0,)), ((), ())), preferred_element_type=jnp.float32
-        ),
-        "seq",
-        scatter_dimension=0,
-        tiled=True,
-    )
-    grad_point = lax.psum(shares.astype(jnp.bfloat16), "utt").astype(jnp.float32)
-    return (
-        layer_out[None],
-        grad_hidden[None],
-        grad_point * grad_scale,
-        summed_kernel * grad_scale,
-        summed_gain * grad_scale,
-    )
+    return layer_out[None], grad_hidden[None], grad_point, grad_kernel, grad_gain[0]
 
 
 def solution(mesh):

time: 289 us -> 102 us (0.35)
  waiting for transfers between devices: 109 us -> 0 us
  blocking collectives: 71.4 us -> 0 us
  Pallas kernels: 42.5 us -> 89.2 us
  other arithmetic: 17.8 us -> 1.31 us
  between operations: 15.9 us -> 0.66 us
  matrix products: 12.6 us -> 0 us
  starting transfers between devices: 11 us -> 0 us
    reduce_scatter x1 -> x0, waiting for transfers between devices: 81.9 us -> none  [on_device(): lax.psum_scatter(lax.dot_general(act, grad_now, (((0,), (0,)), ((), ())),...]
    psum x1 -> x0, blocking collectives: 71.4 us -> none  [on_device(): lax.psum((local_kernel, local_gain), ('seq', 'utt'))]
    pallas_call x1 -> x2, Pallas kernels: 42.5 us -> 89.2 us  [the longest x1 45.2 us: attention(): pl.pallas_call(attention_kernel, name='attention', out_shape=(jax.ShapeDt...]
    psum x2 -> x0, waiting for transfers between devices: 24.3 us -> none  [the longest x1 24.2 us: on_device(): lax.psum(shares.astype(jnp.bfloat16), 'utt').astype(jnp.float32)]
    dot_general x3 -> x0, matrix products: 12.6 us -> none  [the longest x1 5.87 us: on_device(): lax.dot_general(grad_now, w_point, (((1,), (1,)), ((), ())), preferred_el...]
    ppermute x4 -> x0, starting transfers between devices: 10.9 us -> none  [the longest x2 6.57 us: with_halo(): lax.ppermute(lax.slice_in_dim(block, block.shape[dim] - width, None, axis...]
    reduce_sum x4 -> x0, other arithmetic: 7.12 us -> none  [the longest x1 5.2 us: on_device(): local_gain = jnp.sum(dconv_in * hhat, axis=0)]
    mul x3 -> x0, other arithmetic: 3.77 us -> none  [the longest x1 1.62 us: on_device(): summed_kernel * grad_scale]
  transfers between devices with their start and end apart: 7 -> 0, of which waited for: 3 -> 0; matrix products, arithmetic and copies ran while one was open for 8% -> 0% of each run, Pallas kernels for 0% -> 0%
where the time goes in v2:
time: 102 us; the launch traced here: 101 us
  Pallas kernels  89.2 us (87%)
  local copies, waits for them, and re-layouts  10.1 us (10%)
  other arithmetic  1.31 us (1%)
    pallas_call x1, Pallas kernels, attention(): pl.pallas_call(attention_kernel, name='attention', out_shape=(jax.ShapeDt...  45.2 us
    pallas_call x1, Pallas kernels, conv_module(): pl.pallas_call(conv_kernel, name='conv_module', out_shape=tuple((jax.Shap...  44.1 us
    unnamed x6, local copies, waits for them, and re-layouts  6.74 us

profile of v2, /device:TPU:1, one launch (start us, length us, event | category | flops | bytes accessed | tf_op | source)
XLA Modules:
  0.0 101.3 jit_solution(14702532569559116278)
XLA Ops:
  0.6 0.0 copy-start
  0.6 1.3 %broadcast_in_dim.12.gain_ref = f32[1,1536]{1,0:T(1,128)} reshape(f32[1536]{0:T(1024)} %param.11) | data formatting | bytes 12288 | tf_op jit(solution)/shard_map/broadcast_in_dim | solution.py:516
  2.0 1.3 %broadcast_in_dim.13.gain_ref = f32[1,1536]{1,0:T(1,128)} reshape(f32[1536]{0:T(1024)} %param.16) | data formatting | bytes 12288 | tf_op jit(solution)/shard_map/broadcast_in_dim | solution.py:520
  3.3 0.0 copy-done
  3.3 0.7 bitcast_bitcast_fusion.taps_ref
  4.0 45.2 %attention.1 = (bf16[128,1536]{1,0:T(8,128)(2,1)}, bf16[1024,1536]{1,0:T(8,128)(2,1)}) custom-call(bf16[128,1536]{1,0:T(8,128)(2,1)} %bitcast.13, f32[1,1536]{1,0:T(1,128)} %broadcast_in_dim.12.gain_ref, bf16[1536,768]{1,0:T(8,128)(2,1)} %wk_hbm.1, bf16[1536,768]{1,0:T(8,128)(2,1)} %wv_hbm.1, bf16[1536,768]{1,0:T(8,128)(2,1)} %wq_hbm.1, ...), custom_call_target="tpu_custom_call" | custom-call | flops 6000000000 | bytes 10485760 | tf_op jit(solution)/shard_map/attention/pallas_call | solution.py:220
  49.1 44.1 %conv_module.1 = (bf16[128,1536]{1,0:T(8,128)(2,1)}, bf16[128,1536]{1,0:T(8,128)(2,1)}, f32[24,1536]{1,0:T(8,128)}, f32[32,1536]{1,0:T(8,128)}, f32[1,1536]{1,0:T(1,128)}) custom-call(bf16[128,1536]{1,0:T(8,128)(2,1)} %get-tuple-element.12.hidden_ref, f32[1,1536]{1,0:T(1,128)} %broadcast_in_dim.13.gain_ref, f32[12,32,128]{2,1,0:T(8,128)} %bitcast_bitcast_fusion.taps_ref, ...), custom_call_target="tpu_custom_call" | custom-call | flops 3000000000 | bytes 10485760 | tf_op jit(solution)/shard_map/conv_module/pallas_call | solution.py:461
  93.2 1.3 %reduce = f32[1536]{0:T(1024)} reduce(f32[1,1536]{1,0:T(1,128)} %get-tuple-element.18, f32[]{:T(128)} %constant.2), dimensions={0}, to_apply=%get-tuple-element.18.reduce_sub_computation | reduce | bytes 12292 | tf_op jit(solution)/shard_map/conv_module/pallas_call | solution.py:461
  94.5 1.8 %copy.22 = bf16[1,128,1536]{2,1,0:T(8,128)(2,1)} copy(bf16[1,128,1536]{2,1,0:T(8,128)(2,1)} %bitcast.12) | data formatting | bytes 786432
  96.3 1.8 %copy.23 = bf16[1,128,1536]{2,1,0:T(8,128)(2,1)} copy(bf16[1,128,1536]{2,1,0:T(8,128)(2,1)} %bitcast.11) | data formatting | bytes 786432
  98.1 1.6 %copy.24 = f32[24,1536]{1,0:T(8,128)} copy(f32[24,1536]{1,0:T(8,128)} %get-tuple-element.26) | data formatting | bytes 294912
  99.7 1.6 %copy.25 = f32[32,1536]{1,0:T(8,128)} copy(f32[32,1536]{1,0:T(8,128)} %get-tuple-element.27) | data formatting | bytes 393216
Async XLA Ops:
  0.6 2.6 %copy-start = (f32[32,1536]{1,0:T(8,128)S(1)}, f32[32,1536]{1,0:T(8,128)}, u32[]{:S(2)}) copy-start(f32[32,1536]{1,0:T(8,128)} %param.17) | copy-start | bytes 589828

commit v3 on v2

--- a/solution.py
+++ b/solution.py
@@ -34,7 +34,7 @@
     x_ref, gain_ref, wk_hbm, wv_hbm, wq_hbm, wo_hbm, cot_hbm,
     hidden_ref, cots_hbm,
     wk, wv, wq, wo, normed, kv_out, q_out, kv, qt, acc, top, mix_out, mixt,
-    wsem, kv_send, kv_recv, q_send, q_recv, m_send, m_recv, r_send, r_recv, c_send, c_recv, lsem,
+    wsem, kv_send, kv_recv, q_send, q_recv, m_send, m_recv, r_send, r_recv, c_send, c_recv,
 ):
     s = lax.axis_index("seq")
     z = s // 16
@@ -87,8 +87,7 @@
                kv_send.at[k - 1], kv_recv.at[k - 1], peers[k - 1])
         for k in range(1, 8)
     ]
-    kv_self = pltpu.make_async_copy(kv_out.at[h], kv.at[h // 4, 0:192, mine], lsem.at[0])
-    kv_self.start()
+    kv[h // 4, 0:192, mine] = kv_out[h]
 
     loads[2].wait()
     scale = LOG2E / math.sqrt(HEAD_DIM)
@@ -101,8 +100,7 @@
                q_send.at[k - 1], q_recv.at[k - 1], peers[k - 1])
         for k in range(1, 8)
     ]
-    q_self = pltpu.make_async_copy(q_out.at[h], qt.at[:, lanes], lsem.at[1])
-    q_self.start()
+    qt[:, lanes] = q_out[h]
 
     sent = []
 
@@ -131,7 +129,6 @@
 
     for copy in kv_copies:
         copy.wait_recv()
-    kv_self.wait()
     zm0 = forward(OWN, 0, up, ZM)
     zp1 = forward(OWN, 1, down, ZP)
     sib0 = forward(OWN, 0, sibling, SIB)
@@ -140,8 +137,6 @@
     zp0 = forward(OWN, 0, down, ZP)
     x, side = h % 4, h // 4
     own_rows = pl.ds(pl.multiple_of((x * 2 + c) * BLOCK, BLOCK), BLOCK)
-    c_self = pltpu.make_async_copy(cot_hbm, cots_hbm.at[own_rows], lsem.at[3])
-    c_self.start()
     c_copies = [
         remote(cot_hbm, cots_hbm.at[own_rows], c_send.at[k - 1], c_recv.at[k - 1],
                dev(z, side * 4 + (x + k) % 4, c))
@@ -152,7 +147,6 @@
     )
     for copy in q_copies:
         copy.wait_recv()
-    q_self.wait()
     attend((OWN, 0), (OWN, 1))
     zm0.wait_recv()
     z20 = forward(ZM, 0, up, Z2)
@@ -196,18 +190,15 @@
             remote(mix_out.at[:, to_lanes], mixt.at[band, :],
                    m_send.at[k - 1], m_recv.at[k - 1], peers[k - 1])
         )
-    m_self = pltpu.make_async_copy(mix_out.at[:, lanes], mixt.at[band, :], lsem.at[2])
-    m_self.start()
+    mixt[band, :] = mix_out[:, lanes]
     loads[3].wait()
     for copy in m_copies:
         copy.wait_recv()
-    m_self.wait()
     hidden_ref[...] = (x_ref[...].astype(jnp.float32) + matmul(mixt[...], wo[...], 0, 0)).astype(
         jnp.bfloat16
     )
     for copy in c_copies[3:]:
         copy.wait_recv()
-    c_self.wait()
     for copy in kv_copies + q_copies + sent + m_copies + c_copies:
         copy.wait_send()
 
@@ -238,7 +229,7 @@
             pltpu.VMEM((96, 1024), bf),
             pltpu.VMEM((WIDE, 128), bf),
             dma((4,)), dma((7,)), dma((7,)), dma((7,)), dma((7,)), dma((7,)), dma((7,)),
-            dma((14,)), dma((14,)), dma((7,)), dma((7,)), dma((4,)),
+            dma((14,)), dma((14,)), dma((7,)), dma((7,)),
         ],
         compiler_params=pltpu.CompilerParams(
             collective_id=0, has_side_effects=True, vmem_limit_bytes=60 << 20
@@ -281,8 +272,13 @@
 
     wp_load = pltpu.make_async_copy(wp_hbm, wp, lsem.at[0])
     wp_load.start()
-    cots_load = pltpu.make_async_copy(cots_hbm, cots, lsem.at[1])
-    cots_load.start()
+    own_rows = pl.ds(pl.multiple_of(p * BLOCK, BLOCK), BLOCK)
+    cots_loads = []
+    for k in range(1, 8):
+        rows = pl.ds(pl.multiple_of((p + k) % 8 * BLOCK, BLOCK), BLOCK)
+        cots_loads.append(pltpu.make_async_copy(cots_hbm.at[rows], cots.at[rows], lsem.at[k]))
+        cots_loads[-1].start()
+    cots[own_rows, :] = cot_ref[...]
     barrier = pltpu.get_barrier_semaphore()
     for to in [right, left] + group + z_peers + y_peers:
         pl.semaphore_signal(barrier, inc=1, device_id=to, device_id_type=pl.DeviceIdType.MESH)
@@ -352,8 +348,7 @@
                a_send.at[k - 1], a_recv.at[k - 1], group[k - 1])
         for k in range(1, 8)
     ]
-    act_self = pltpu.make_async_copy(act_out.at[p], act_in.at[:, own_lanes], lsem.at[2])
-    act_self.start()
+    act_in[:, own_lanes] = act_out[p]
     out_ref[...] = (hidden_ref[...].astype(f32) + matmul(act[...], wp[...])).astype(bf)
 
     for copy in halo:
@@ -385,8 +380,8 @@
 
     for copy in act_copies:
         copy.wait_recv()
-    act_self.wait()
-    cots_load.wait()
+    for load in cots_loads:
+        load.wait()
     tile = matmul(act_in[...], cots[...])
     for b in range(4):
         tile_out[b] = tile[48 * b : 48 * b + 48, :].astype(bf)
@@ -487,7 +482,7 @@
             pltpu.VMEM((4, 64, 128), f32),
             pltpu.VMEM((4, 64, 128), f32),
             pltpu.VMEM((512, 128), f32),
-            dma((3,)), dma((4,)), dma((4,)), dma((7,)), dma((7,)), dma((7,)), dma((7,)),
+            dma((8,)), dma((4,)), dma((4,)), dma((7,)), dma((7,)), dma((7,)), dma((7,)),
             dma((3,)), dma((3,)), dma((3,)), dma((3,)), dma((7,)), dma((7,)),
             dma((3,)), dma((3,)), dma((3,)), dma((3,)),
         ],

time: 102 us -> 102 us (level)
  no operation moved by 1% of the time
where the time goes in v3:
time: 102 us; the launch traced here: 101 us
  Pallas kernels  89.4 us (88%)
  local copies, waits for them, and re-layouts  10.1 us (10%)
  other arithmetic  1.31 us (1%)
    pallas_call x1, Pallas kernels, attention(): pl.pallas_call(attention_kernel, name='attention', out_shape=(jax.ShapeDt...  45.1 us
    pallas_call x1, Pallas kernels, conv_module(): pl.pallas_call(conv_kernel, name='conv_module', out_shape=tuple((jax.Shap...  44.3 us
    unnamed x6, local copies, waits for them, and re-layouts  6.74 us

profile of v3, /device:TPU:1, one launch (start us, length us, event | category | flops | bytes accessed | tf_op | source)
XLA Modules:
  0.0 101.4 jit_solution(13140075983157560958)
XLA Ops:
  0.6 0.0 copy-start
  0.6 1.3 %broadcast_in_dim.12.gain_ref = f32[1,1536]{1,0:T(1,128)} reshape(f32[1536]{0:T(1024)} %param.11) | data formatting | bytes 12288 | tf_op jit(solution)/shard_map/broadcast_in_dim | solution.py:511
  2.0 1.3 %broadcast_in_dim.13.gain_ref = f32[1,1536]{1,0:T(1,128)} reshape(f32[1536]{0:T(1024)} %param.16) | data formatting | bytes 12288 | tf_op jit(solution)/shard_map/broadcast_in_dim | solution.py:515
  3.3 0.0 copy-done
  3.3 0.7 bitcast_bitcast_fusion.taps_ref
  4.0 45.1 %attention.1 = (bf16[128,1536]{1,0:T(8,128)(2,1)}, bf16[1024,1536]{1,0:T(8,128)(2,1)}) custom-call(bf16[128,1536]{1,0:T(8,128)(2,1)} %bitcast.13, f32[1,1536]{1,0:T(1,128)} %broadcast_in_dim.12.gain_ref, bf16[1536,768]{1,0:T(8,128)(2,1)} %wk_hbm.1, bf16[1536,768]{1,0:T(8,128)(2,1)} %wv_hbm.1, bf16[1536,768]{1,0:T(8,128)(2,1)} %wq_hbm.1, ...), custom_call_target="tpu_custom_call" | custom-call | flops 6000000000 | bytes 10485760 | tf_op jit(solution)/shard_map/attention/pallas_call | solution.py:211
  49.1 44.3 %conv_module.1 = (bf16[128,1536]{1,0:T(8,128)(2,1)}, bf16[128,1536]{1,0:T(8,128)(2,1)}, f32[24,1536]{1,0:T(8,128)}, f32[32,1536]{1,0:T(8,128)}, f32[1,1536]{1,0:T(1,128)}) custom-call(bf16[128,1536]{1,0:T(8,128)(2,1)} %get-tuple-element.12.hidden_ref, f32[1,1536]{1,0:T(1,128)} %broadcast_in_dim.13.gain_ref, f32[12,32,128]{2,1,0:T(8,128)} %bitcast_bitcast_fusion.taps_ref, ...), custom_call_target="tpu_custom_call" | custom-call | flops 3000000000 | bytes 10485760 | tf_op jit(solution)/shard_map/conv_module/pallas_call | solution.py:456
  93.4 1.3 %reduce = f32[1536]{0:T(1024)} reduce(f32[1,1536]{1,0:T(1,128)} %get-tuple-element.18, f32[]{:T(128)} %constant.2), dimensions={0}, to_apply=%get-tuple-element.18.reduce_sub_computation | reduce | bytes 12292 | tf_op jit(solution)/shard_map/conv_module/pallas_call | solution.py:456
  94.7 1.8 %copy.22 = bf16[1,128,1536]{2,1,0:T(8,128)(2,1)} copy(bf16[1,128,1536]{2,1,0:T(8,128)(2,1)} %bitcast.12) | data formatting | bytes 786432
  96.5 1.8 %copy.23 = bf16[1,128,1536]{2,1,0:T(8,128)(2,1)} copy(bf16[1,128,1536]{2,1,0:T(8,128)(2,1)} %bitcast.11) | data formatting | bytes 786432
  98.2 1.6 %copy.24 = f32[24,1536]{1,0:T(8,128)} copy(f32[24,1536]{1,0:T(8,128)} %get-tuple-element.26) | data formatting | bytes 294912
  99.8 1.6 %copy.25 = f32[32,1536]{1,0:T(8,128)} copy(f32[32,1536]{1,0:T(8,128)} %get-tuple-element.27) | data formatting | bytes 393216
Async XLA Ops:
  0.6 2.6 %copy-start = (f32[32,1536]{1,0:T(8,128)S(1)}, f32[32,1536]{1,0:T(8,128)}, u32[]{:S(2)}) copy-start(f32[32,1536]{1,0:T(8,128)} %param.17) | copy-start | bytes 589828

commit v4 on v0

v4 whole, which is shorter than its diff:
```python
import math

import jax
import jax.numpy as jnp
from jax import lax
from jax.experimental import pallas as pl
from jax.experimental.pallas import tpu as pltpu
from jax.sharding import PartitionSpec as P

D = 1536
HEADS = 8
HEAD_DIM = 96
WIDE = HEADS * HEAD_DIM
KER = 32
BLOCK = 128
HALF = 512
LOG2E = 1.4426950408889634

OWN, SIB, ZM, ZP, Z2, SIB_ZM, SIB_ZP, SIB_Z2 = range(8)


def rows_norm(values):
    mean = jnp.mean(values, axis=-1, keepdims=True)
    centered = values - mean
    rstd = lax.rsqrt(jnp.mean(centered * centered, axis=-1, keepdims=True) + 1e-05)
    return centered * rstd, rstd


def matmul(a, b, da=1, db=0):
    return lax.dot_general(a, b, (((da,), (db,)), ((), ())), preferred_element_type=jnp.float32)


def layer_kernel(
    x_ref, gain_ref, wk_hbm, wv_hbm, wq_hbm, wo_hbm, gain_conv_ref, taps_ref, wp_hbm, cot_ref,
    out_ref, gh_ref, gp_ref, gk_ref, gg_ref,
    wk, wv, wq, wo, wp, normed, kv_out, q_out, kv, qt, acc, top, mix_out, mixt, cots,
    hidden, hhat, ci, back, dz, conv, act, act_t, act_out, act_in, edge, halo, tile_out, tile_in,
    y_out, y_in, part, sums, b_out, b_in, c_in, d_in, total,
    w_sem, kv_send, kv_recv, q_send, q_recv, m_send, m_recv, r_send, r_recv, s_send, s_recv,
    e_send, e_recv, a_send, a_recv, b_send, b_recv, c_send, c_recv, d_send, d_recv,
    g_send, g_recv, t_send, t_recv, y_send, y_recv,
):
    f32, bf = jnp.float32, jnp.bfloat16
    s = lax.axis_index("seq")
    u = lax.axis_index("utt")
    z, y_hi, x, c = s // 16, (s // 8) % 2, (s // 2) % 4, s % 2
    h, p, y = y_hi * 4 + x, s % 8, y_hi * 2 + u

    def dev(zz, hh, cc):
        return {"seq": zz * 16 + hh * 2 + cc}

    def plane(side, step, sign=1):
        return (y_hi + side) % 2 * 4 + (x + sign * step + 4) % 4

    near = [(0, 1), (0, 2), (0, 3)]
    away = [(1, 0), (1, 1), (1, 2), (1, 3)]
    up, down, sibling = dev((z + 1) % 4, h, c), dev((z + 3) % 4, h, c), dev(z, h, 1 - c)
    right, left = {"seq": (s + 1) % 64}, {"seq": (s + 63) % 64}
    group = [{"seq": s // 8 * 8 + (p + k) % 8} for k in range(1, 8)]
    z_peers = [dev((z + k) % 4, h, c) for k in range(1, 4)]
    y_peers = [
        {"seq": z * 16 + (y + k) % 4 // 2 * 8 + p, "utt": (y + k) % 4 % 2} for k in range(1, 4)
    ]
    copies = []

    def remote(src, dst, send, recv, to):
        copy = pltpu.make_async_remote_copy(
            src_ref=src, dst_ref=dst, send_sem=send, recv_sem=recv,
            device_id=to, device_id_type=pl.DeviceIdType.MESH,
        )
        copy.start()
        copies.append(copy)
        return copy

    def arrive(group_of_copies):
        for copy in group_of_copies:
            copy.wait_recv()

    loads = {}
    sem = 0
    for name, src, dst, cuts in (
        ("k", wk_hbm, wk, 2), ("v", wv_hbm, wv, 2), ("q", wq_hbm, wq, 2),
        ("p", wp_hbm, wp, 2), ("o", wo_hbm, wo, 2),
    ):
        rows = dst.shape[0] // cuts
        loads[name] = []
        for i in range(cuts):
            cut = pl.ds(i * rows, rows)
            loads[name].append(pltpu.make_async_copy(src.at[cut], dst.at[cut], w_sem.at[sem]))
            loads[name][-1].start()
            sem += 1

    def loaded(name):
        for load in loads[name]:
            load.wait()

    for slot in range(16):
        kv[slot, 192:208, :] = jnp.ones((16, HALF), bf)
    barrier = pltpu.get_barrier_semaphore()
    greeted = [dev(z, plane(a, b), c) for a, b in near + away] + group + z_peers + y_peers
    greeted += [right, left]
    for to in greeted:
        pl.semaphore_signal(barrier, inc=1, device_id=to, device_id_type=pl.DeviceIdType.MESH)

    xhat, unused_item = rows_norm(x_ref[...].astype(f32))
    normed[...] = (xhat * gain_ref[...].reshape(1, D)).astype(bf)
    loaded("k")
    rows = matmul(normed[...], wk[...]).T.astype(bf)
    for i in range(HEADS):
        kv_out[i, 0:96, :] = rows[i * 96 : i * 96 + 96, :]
    loaded("v")
    rows = matmul(normed[...], wv[...]).T.astype(bf)
    for i in range(HEADS):
        kv_out[i, 96:192, :] = rows[i * 96 : i * 96 + 96, :]
    pl.semaphore_wait(barrier, len(greeted))
    mine = pl.ds(pl.multiple_of(x * 128, 128), 128)
    lanes = pl.ds(pl.multiple_of(h * 128, 128), 128)

    def exchange(src, dst, send, recv, peers):
        made = []
        for a, b in peers:
            to = plane(a, b)
            made.append(remote(src(to), dst, send.at[4 * a + b], recv.at[4 * a + b], dev(z, to, c)))
        return made

    kv_near = exchange(lambda i: kv_out.at[i], kv.at[y_hi, 0:192, mine], kv_send, kv_recv, near)
    kv_away = exchange(lambda i: kv_out.at[i], kv.at[y_hi, 0:192, mine], kv_send, kv_recv, away)
    kv[y_hi, 0:192, mine] = kv_out[h]
    loaded("q")
    rows = (matmul(normed[...], wq[...]) * (LOG2E / math.sqrt(HEAD_DIM))).T.astype(bf)
    for i in range(HEADS):
        q_out[i] = rows[i * 96 : i * 96 + 96, :]
    q_near = exchange(lambda i: q_out.at[i], qt.at[:, lanes], q_send, q_recv, near)
    q_away = exchange(lambda i: q_out.at[i], qt.at[:, lanes], q_send, q_recv, away)
    qt[:, lanes] = q_out[h]
    acc[...] = jnp.zeros_like(acc)
    top[...] = jnp.full_like(top, -1e30)

    NEAR, AWAY = y_hi, 1 - y_hi
    hops = []

    def forward(slot, half, to, to_slot):
        i = len(hops)
        copy = remote(kv.at[2 * slot + half, 0:192], kv.at[2 * to_slot + half, 0:192],
                      r_send.at[i], r_recv.at[i], to)
        hops.append(copy)
        return copy

    def attend(side, *halves):
        span = pl.ds(pl.multiple_of(side * HALF, HALF), HALF)
        halves = [2 * slot + half for slot, half in halves]
        scores = [matmul(kv[i, 0:96, :], qt[:, span], 0, 0) for i in halves]
        before = top[0:1, span]
        newest = before
        for one in scores:
            newest = jnp.maximum(newest, jnp.max(one, axis=0, keepdims=True))
        result = acc[:, span] * jnp.exp2(before - newest)
        for i, one in zip(halves, scores):
            result += matmul(kv[i, 96:208, :], jnp.exp2(one - newest).astype(bf))
        acc[:, span] = result
        top[0:1, span] = newest

    def attend_both(*halves):
        def one_side(side, carry):
            attend(side, *halves)
            return carry

        lax.fori_loop(0, 2, one_side, 0)

    arrive(kv_near)
    zm_n = forward(OWN, NEAR, up, ZM)
    zp_n = forward(OWN, NEAR, down, ZP)
    sib_n = forward(OWN, NEAR, sibling, SIB)
    loaded("p")
    grads = matmul(cot_ref[...], wp[...], 1, 1)
    for l in range(12):
        back[l] = grads[:, l * 128 : l * 128 + 128]
    arrive(kv_away)
    zp_a = forward(OWN, AWAY, down, ZP)
    zm_a = forward(OWN, AWAY, up, ZM)
    sib_a = forward(OWN, AWAY, sibling, SIB)
    arrive(q_near)
    sib_n.wait_recv()
    attend(NEAR, (OWN, NEAR), (SIB, NEAR))
    arrive(q_away)
    own_rows = pl.ds(pl.multiple_of(p * BLOCK, BLOCK), BLOCK)
    cots[own_rows, :] = cot_ref[...]
    cot_copies = [
        remote(cot_ref, cots.at[own_rows], s_send.at[k], s_recv.at[k], dev(z, plane(0, k), c))
        for k in range(1, 4)
    ]
    cot_copies.append(remote(cot_ref, cots.at[own_rows], s_send.at[0], s_recv.at[0], sibling))
    attend(AWAY, (OWN, NEAR), (SIB, NEAR))
    sib_a.wait_recv()
    attend_both((OWN, AWAY), (SIB, AWAY))
    zm_n.wait_recv()
    z2_n = forward(ZM, NEAR, up, Z2)
    szm_n = forward(ZM, NEAR, sibling, SIB_ZM)
    zp_n.wait_recv()
    szp_n = forward(ZP, NEAR, sibling, SIB_ZP)
    attend_both((ZM, NEAR), (ZP, NEAR))
    zp_a.wait_recv()
    z2_a = forward(ZP, AWAY, down, Z2)
    szp_a = forward(ZP, AWAY, sibling, SIB_ZP)
    zm_a.wait_recv()
    szm_a = forward(ZM, AWAY, sibling, SIB_ZM)
    arrive([szm_n, szp_n])
    attend_both((SIB_ZM, NEAR), (SIB_ZP, NEAR), (ZM, AWAY), (ZP, AWAY))
    z2_n.wait_recv()
    sz2_n = forward(Z2, NEAR, sibling, SIB_Z2)
    z2_a.wait_recv()
    sz2_a = forward(Z2, AWAY, sibling, SIB_Z2)
    arrive([szm_a, szp_a])
    attend_both((SIB_ZM, AWAY), (SIB_ZP, AWAY), (Z2, NEAR), (Z2, AWAY))
    arrive(cot_copies)
    cot_relays = []
    for k in range(1, 4):
        rows = pl.ds(pl.multiple_of((plane(0, k, -1) % 4 * 2 + c) * BLOCK, BLOCK), BLOCK)
        cot_relays.append(
            remote(cots.at[rows], cots.at[rows], s_send.at[3 + k], s_recv.at[3 + k], sibling)
        )
    arrive([sz2_n, sz2_a])
    band = pl.ds(pl.multiple_of(h * 96, 96), 96)

    def give_back(side, peers):
        span = pl.ds(pl.multiple_of(side * HALF, HALF), HALF)
        mix_out[:, span] = (acc[0:96, span] / acc[96:97, span]).astype(bf)
        return exchange(
            lambda i: mix_out.at[:, pl.ds(pl.multiple_of(i * 128, 128), 128)],
            mixt.at[band, :], m_send, m_recv, peers,
        )

    attend(AWAY, (SIB_Z2, NEAR), (SIB_Z2, AWAY))
    m_away = give_back(AWAY, away)
    attend(NEAR, (SIB_Z2, NEAR), (SIB_Z2, AWAY))
    m_near = give_back(NEAR, near)
    mixt[band, :] = mix_out[:, lanes]
    loaded("o")
    arrive(m_away + m_near)
    hidden[...] = (x_ref[...].astype(f32) + matmul(mixt[...], wo[...], 0, 0)).astype(bf)

    standard, rstd = rows_norm(hidden[...].astype(f32))
    conv_in = (standard * gain_conv_ref[...].reshape(1, D)).astype(bf)
    edge[0] = conv_in[BLOCK - 16 :, :]
    edge[1] = conv_in[:16, :]
    halos = [
        remote(edge.at[0], halo.at[0], e_send.at[0], e_recv.at[0], right),
        remote(edge.at[1], halo.at[1], e_send.at[1], e_recv.at[1], left),
    ]
    for l in range(12):
        hhat[l] = standard[:, l * 128 : l * 128 + 128]
        ci[l, 16:144, :] = conv_in[:, l * 128 : l * 128 + 128].astype(f32)
    sums[480:512, :] = jnp.zeros((32, 128), f32)

    def place_halo(ref, slot):
        low = jnp.where(s > 0, halo[slot].astype(f32), 0.0)
        high = jnp.where(s < 63, halo[slot + 1].astype(f32), 0.0)
        for l in range(12):
            ref[l, 0:16, :] = low[:, l * 128 : l * 128 + 128]
            ref[l, 144:160, :] = high[:, l * 128 : l * 128 + 128]

    def span_of(l):
        return pl.ds(pl.multiple_of(l * 128, 128), 128)

    def conv_rows(l, first, count):
        result = jnp.zeros((count, 128), f32)
        for j in range(KER):
            result += taps_ref[j : j + 1, span_of(l)] * ci[l, first + j : first + j + count, :]
        conv[l, first : first + count, :] = result

    def grad_rows(l, first, count):
        result = jnp.zeros((count, 128), f32)
        for j in range(KER):
            start = first + 32 - j
            result += taps_ref[j : j + 1, span_of(l)] * dz[l, start : start + count, :]
        return result

    def middle(l, carry):
        conv_rows(l, 16, 96)
        return carry

    lax.fori_loop(0, 12, middle, 0)
    arrive(halos)
    place_halo(ci, 0)

    def activate(l, carry):
        conv_rows(l, 0, 16)
        conv_rows(l, 112, 16)
        value = conv[l]
        sig = 1.0 / (1.0 + jnp.exp(-value))
        rounded = (value * sig).astype(bf)
        act[:, span_of(l)] = rounded
        act_t[span_of(l), :] = rounded.astype(f32).T
        dz[l, 16:144, :] = back[l] * (sig * (1.0 + value * (1.0 - sig)))
        return carry

    lax.fori_loop(0, 12, activate, 0)
    for l in range(12):
        edge[2, :, l * 128 : l * 128 + 128] = dz[l, 128:144, :].astype(bf)
        edge[3, :, l * 128 : l * 128 + 128] = dz[l, 16:32, :].astype(bf)
    halos = [
        remote(edge.at[2], halo.at[2], e_send.at[2], e_recv.at[2], right),
        remote(edge.at[3], halo.at[3], e_send.at[3], e_recv.at[3], left),
    ]
    for i in range(8):
        pieces = [act_t[24 * (8 * b + i) : 24 * (8 * b + i) + 24, :] for b in range(8)]
        act_out[i] = jnp.concatenate(pieces, axis=0).astype(bf)
    own_lanes = pl.ds(pl.multiple_of(p * 128, 128), 128)
    act_copies = [
        remote(act_out.at[(p + k) % 8], act_in.at[:, own_lanes],
               a_send.at[k - 1], a_recv.at[k - 1], group[k - 1])
        for k in range(1, 8)
    ]
    act_in[:, own_lanes] = act_out[p]

    def taps_grad(l, carry):
        grad = dz[l, 16:144, :]
        for j0 in range(0, KER, 8):
            rows = [
                jnp.sum(grad * ci[l, j : j + BLOCK, :], axis=0, keepdims=True)
                for j in range(j0, j0 + 8)
            ]
            sums[pl.ds(pl.multiple_of(l * 40 + j0, 8), 8), :] = jnp.concatenate(rows, axis=0)
        return carry

    lax.fori_loop(0, 12, taps_grad, 0)

    arrive(halos)
    place_halo(dz, 2)
    part[...] = jnp.zeros_like(part)

    def backward(l, carry):
        grad = grad_rows(l, 0, BLOCK)
        row = jnp.sum(grad * hhat[l], axis=0, keepdims=True)
        sums[pl.ds(pl.multiple_of(l * 40 + 32, 8), 8), :] = jnp.concatenate(
            [row, jnp.zeros((7, 128), f32)], axis=0
        )
        g = grad * gain_conv_ref[span_of(l)].reshape(1, 128)
        back[l] = g
        part[0] += g
        part[1] += g * hhat[l]
        return carry

    lax.fori_loop(0, 12, backward, 0)
    b_out[...] = sums[...].astype(bf)
    b_copies = [
        remote(b_out.at[pl.ds(pl.multiple_of((p + k) % 8 * 64, 64), 64)], b_in.at[k - 1],
               b_send.at[k - 1], b_recv.at[k - 1], group[k - 1])
        for k in range(1, 8)
    ]

    arrive(act_copies)
    arrive(cot_relays)
    t_copies = []
    for i in range(2):
        tile = matmul(act_in[...], cots[:, i * 768 : i * 768 + 768])
        for b in range(4):
            tile_out[i, b] = tile[48 * b : 48 * b + 48, :].astype(bf)
        t_copies.append([
            remote(tile_out.at[i, (z + k) % 4], tile_in.at[i, k - 1],
                   t_send.at[3 * i + k - 1], t_recv.at[3 * i + k - 1], z_peers[k - 1])
            for k in range(1, 4)
        ])
    arrive(b_copies)
    own = pl.ds(pl.multiple_of(p * 64, 64), 64)
    c_in[z] = (sums[own, :] + sum(b_in[k].astype(f32) for k in range(7))).astype(bf)
    c_copies = [
        remote(c_in.at[z], c_in.at[z], c_send.at[k], c_recv.at[k], z_peers[k]) for k in range(3)
    ]
    out_ref[...] = (hidden[...].astype(f32) + matmul(act[...], wp[...])).astype(bf)
    arrive(c_copies)
    d_in[y] = sum(c_in[k].astype(f32) for k in range(4)).astype(bf)
    d_copies = [
        remote(d_in.at[y], d_in.at[y], d_send.at[k], d_recv.at[k], y_peers[k]) for k in range(3)
    ]
    mean_g = jnp.sum(part[0], axis=-1, keepdims=True) * (1.0 / D)
    mean_gh = jnp.sum(part[1], axis=-1, keepdims=True) * (1.0 / D)
    for l in range(12):
        cut = slice(l * 128, l * 128 + 128)
        inner = back[l] - mean_g - hhat[l] * mean_gh
        gh_ref[:, cut] = (cot_ref[:, cut].astype(f32) + rstd * inner).astype(bf)
    y_copies = []

    def along_y(i):
        arrive(t_copies[i])
        mixed = tile_out[i, z].astype(f32) + sum(tile_in[i, k].astype(f32) for k in range(3))
        for b in range(2):
            rows = mixed[24 * b : 24 * b + 24, :]
            y_out[i, b] = jnp.concatenate([rows[:, :384], rows[:, 384:]], axis=0).astype(bf)
        y_copies.append([
            remote(y_out.at[i, (y + k) % 4 // 2], y_in.at[i, y],
                   y_send.at[3 * i + k - 1], y_recv.at[3 * i + k - 1], y_peers[k - 1])
            for k in range(1, 4)
        ])
        y_in[i, y] = y_out[i, y_hi]

    along_y(0)
    arrive(d_copies)
    total[own, :] = sum(d_in[k].astype(f32) for k in range(4)).astype(bf)
    g_copies = [
        remote(total.at[own], total.at[own], g_send.at[k], g_recv.at[k], group[k])
        for k in range(7)
    ]
    along_y(1)
    scale = 1.0 / math.sqrt(2 * 64 * BLOCK)
    for i in range(2):
        arrive(y_copies[i])
        whole = sum(y_in[i, k].astype(f32) for k in range(4)) * scale
        gp_ref[:, i * 768 : i * 768 + 384] = whole[:24, :]
        gp_ref[:, i * 768 + 384 : i * 768 + 768] = whole[24:, :]
    arrive(g_copies)
    for l in range(12):
        cut = slice(l * 128, l * 128 + 128)
        gk_ref[:, cut] = total[l * 40 : l * 40 + 32, :].astype(f32) * scale
        gg_ref[:, cut] = total[l * 40 + 32 : l * 40 + 40, :].astype(f32)[:1, :] * scale
    for copy in copies:
        copy.wait_send()


def finish_kernel(out, gh, gp, gk, gg, out_to, gh_to, gp_to, gk_to, gg_to, sem):
    pairs = ((out, out_to), (gh, gh_to), (gp, gp_to), (gk, gk_to))
    moves = [pltpu.make_async_copy(src, dst, sem.at[i]) for i, (src, dst) in enumerate(pairs)]
    for move in moves:
        move.start()
    gg_to[...] = gg[...].reshape(D)
    for move in moves:
        move.wait()


def layer(x, gain, w_key, w_value, w_query, w_out, gain_conv, taps, w_point, cot):
    bf, f32 = jnp.bfloat16, jnp.float32
    vmem = pl.BlockSpec(memory_space=pltpu.VMEM)
    hbm = pl.BlockSpec(memory_space=pl.ANY)
    dma = pltpu.SemaphoreType.DMA
    shapes = [((BLOCK, D), bf), ((BLOCK, D), bf), ((24, D), f32), ((KER, D), f32)]
    outs = [jax.ShapeDtypeStruct(*shape) for shape in shapes]
    scratch = [
        ((D, WIDE), bf), ((D, WIDE), bf), ((D, WIDE), bf), ((WIDE, D), bf), ((D, D), bf),
        ((BLOCK, D), bf),
        ((HEADS, 192, 128), bf), ((HEADS, 96, 128), bf),
        ((16, 208, HALF), bf), ((96, 1024), bf), ((112, 1024), f32), ((8, 1024), f32),
        ((96, 1024), bf), ((WIDE, 128), bf), ((8 * BLOCK, D), bf),
        ((BLOCK, D), bf), ((12, BLOCK, 128), f32), ((12, 160, 128), f32), ((12, BLOCK, 128), f32),
        ((12, 160, 128), f32), ((12, BLOCK, 128), f32), ((BLOCK, D), bf), ((D, BLOCK), f32),
        ((8, 192, 128), bf), ((192, 1024), bf), ((4, 16, D), bf), ((4, 16, D), bf),
        ((2, 4, 48, 768), bf), ((2, 3, 48, 768), bf), ((2, 2, 48, 384), bf), ((2, 4, 48, 384), bf),
        ((2, BLOCK, 128), f32), ((512, 128), f32), ((512, 128), bf), ((7, 64, 128), bf),
        ((4, 64, 128), bf), ((4, 64, 128), bf), ((512, 128), bf),
    ]
    counts = [10, 8, 8, 8, 8, 8, 8, 14, 14, 7, 7, 4, 4, 7, 7, 7, 7, 3, 3, 3, 3, 7, 7, 6, 6, 6, 6]
    results = pl.pallas_call(
        layer_kernel,
        name="layer",
        out_shape=tuple(outs + [jax.ShapeDtypeStruct((1, D), f32)]),
        in_specs=[vmem, vmem, hbm, hbm, hbm, hbm, vmem, vmem, hbm, vmem],
        out_specs=(vmem,) * 5,
        scratch_shapes=[pltpu.VMEM(*shape) for shape in scratch] + [dma((n,)) for n in counts],
        compiler_params=pltpu.CompilerParams(
            collective_id=0, has_side_effects=True, vmem_limit_bytes=60 << 20
        ),
        cost_estimate=pl.CostEstimate(
            flops=9 * 10**9, bytes_accessed=16 * 2**20, transcendentals=2**23
        ),
    )(x, gain, w_key, w_value, w_query, w_out, gain_conv, taps, w_point, cot)
    return pl.pallas_call(
        finish_kernel,
        name="finish",
        out_shape=tuple(outs + [jax.ShapeDtypeStruct((D,), f32)]),
        in_specs=[vmem] * 5,
        out_specs=(hbm,) * 4 + (vmem,),
        scratch_shapes=[dma((4,))],
    )(*results)


def on_device(
    inputs,
    attention_norm_gain,
    w_query,
    w_key,
    w_value,
    w_out,
    gain_conv,
    kernel,
    w_point,
    cotangent,
):
    layer_out, grad_hidden, grad_point, grad_kernel, grad_gain = layer(
        inputs[0], attention_norm_gain, w_key, w_value, w_query, w_out,
        gain_conv, kernel, w_point, cotangent[0],
    )
    return layer_out[None], grad_hidden[None], grad_point, grad_kernel, grad_gain


def solution(mesh):
    placed = (P("utt", "seq", None), P(), P(), P(), P(), P(), P(), P(), P(), P("utt", "seq", None))
    return jax.shard_map(
        on_device,
        mesh=mesh,
        in_specs=placed,
        out_specs=(P("utt", "seq", None), P("utt", "seq", None), P("seq", None), P(), P()),
        check_vma=False,
    )
```

time: 624 us -> 82.8 us (0.13)
  waiting for transfers between devices: 361 us -> 0 us
  Pallas kernels: 0 us -> 81.8 us
  blocking collectives: 73.4 us -> 0 us
  local copies, waits for them, and re-layouts: 64.7 us -> 0 us
  matrix products: 57.6 us -> 0 us
  other arithmetic: 39.9 us -> 0 us
  between operations: 14.5 us -> 0.8 us
  starting transfers between devices: 10.4 us -> 0 us
    psum x2 -> x0, waiting for transfers between devices: 172 us -> none  [the longest x1 146 us: on_device(): lax.psum((local_kernel, local_gain), ('seq', 'utt'))]
    all_gather x2 -> x0, waiting for transfers between devices: 138 us -> none  [the longest x1 89.4 us: on_device(): lax.all_gather(keys, 'seq', axis=0, tiled=True)]
    pallas_call x0 -> x2, Pallas kernels: none -> 81.8 us  [the longest x1 78.9 us: layer(): pl.pallas_call(layer_kernel, name='layer', out_shape=tuple(outs + [jax.Sh...]
    psum x1 -> x0, blocking collectives: 73.4 us -> none  [on_device(): lax.psum((local_kernel, local_gain), ('seq', 'utt'))]
    dot_general x9 -> x0, matrix products: 57.6 us -> none  [the longest x1 17 us: attend_piece(): jnp.einsum('htf,fhd->thd', expo.astype(jnp.bfloat16), value_heads, prefer...]
    reduce_scatter x1 -> x0, waiting for transfers between devices: 49.7 us -> none  [on_device(): lax.psum_scatter(lax.dot_general(act, grad_now, (((0,), (0,)), ((), ())),...]
    all_gather x2 -> x0, local copies, waits for them, and re-layouts: 33.3 us -> none  [the longest x1 16.6 us: on_device(): lax.all_gather(values, 'seq', axis=0, tiled=True)]
    reduce_sum x6 -> x0, other arithmetic: 25.9 us -> none  [the longest x1 14.2 us: attend_piece(): total = jnp.sum(expo, axis=-1)]
  transfers between devices with their start and end apart: 9 -> 0, of which waited for: 6 -> 0; matrix products, arithmetic and copies ran while one was open for 18% -> 0% of each run, Pallas kernels for 0% -> 0%
where the time goes in v4:
time: 82.8 us; the launch traced here: 82.6 us
  Pallas kernels  81.8 us (99%)
    pallas_call x1, Pallas kernels, layer(): pl.pallas_call(layer_kernel, name='layer', out_shape=tuple(outs + [jax.Sh...  78.9 us
    pallas_call x1, Pallas kernels, layer(): pl.pallas_call(finish_kernel, name='finish', out_shape=tuple(outs + [jax....  2.85 us

profile of v4, /device:TPU:1, one launch (start us, length us, event | category | flops | bytes accessed | tf_op | source)
XLA Modules:
  0.0 82.6 jit_solution(7852934020885600462)
XLA Ops:
  0.6 78.9 %layer.1 = (bf16[128,1536]{1,0:T(8,128)(2,1)}, bf16[128,1536]{1,0:T(8,128)(2,1)}, f32[24,1536]{1,0:T(8,128)}, f32[32,1536]{1,0:T(8,128)}, f32[1,1536]{1,0:T(1,128)}) custom-call(bf16[128,1536]{1,0:T(8,128)(2,1)} %bitcast.4, f32[1536]{0:T(1024)} %gain_ref.1, bf16[1536,768]{1,0:T(8,128)(2,1)} %wk_hbm.1, bf16[1536,768]{1,0:T(8,128)(2,1)} %wv_hbm.1, ...), custom_call_target="tpu_custom_call" | custom-call | flops 8999999488 | bytes 16777216 | tf_op jit(solution)/shard_map/layer/pallas_call | solution.py:451
  79.6 2.9 %finish.1 = (bf16[128,1536]{1,0:T(8,128)(2,1)}, bf16[128,1536]{1,0:T(8,128)(2,1)}, f32[24,1536]{1,0:T(8,128)}, f32[32,1536]{1,0:T(8,128)}, f32[1536]{0:T(1024)}) custom-call(bf16[128,1536]{1,0:T(8,128)(2,1)} %get-tuple-element.15.out, bf16[128,1536]{1,0:T(8,128)(2,1)} %get-tuple-element.16.gh, f32[24,1536]{1,0:T(8,128)} %get-tuple-element.17.gp, ...), custom_call_target="tpu_custom_call" | custom-call | tf_op jit(solution)/shard_map/finish/pallas_call | solution.py:465

commit v5 on v4

--- a/solution.py
+++ b/solution.py
@@ -35,10 +35,11 @@
     out_ref, gh_ref, gp_ref, gk_ref, gg_ref,
     wk, wv, wq, wo, wp, normed, kv_out, q_out, kv, qt, acc, top, mix_out, mixt, cots,
     hidden, hhat, ci, back, dz, conv, act, act_t, act_out, act_in, edge, halo, tile_out, tile_in,
-    y_out, y_in, part, sums, b_out, b_in, c_in, d_in, total,
+    y_out, y_in, part, gain_sum, b_out, b_in, c_in, d_in, total, n_group, n_z, n_y,
+    gh_rows, out_rows,
     w_sem, kv_send, kv_recv, q_send, q_recv, m_send, m_recv, r_send, r_recv, s_send, s_recv,
     e_send, e_recv, a_send, a_recv, b_send, b_recv, c_send, c_recv, d_send, d_recv,
-    g_send, g_recv, t_send, t_recv, y_send, y_recv,
+    g_send, g_recv, t_send, t_recv, y_send, y_recv, n_send, n_recv, o_sem,
 ):
     f32, bf = jnp.float32, jnp.bfloat16
     s = lax.axis_index("seq")
@@ -87,7 +88,8 @@
         for i in range(cuts):
             cut = pl.ds(i * rows, rows)
             loads[name].append(pltpu.make_async_copy(src.at[cut], dst.at[cut], w_sem.at[sem]))
-            loads[name][-1].start()
+            if name in "kvq":
+                loads[name][-1].start()
             sem += 1
 
     def loaded(name):
@@ -127,6 +129,8 @@
     kv_away = exchange(lambda i: kv_out.at[i], kv.at[y_hi, 0:192, mine], kv_send, kv_recv, away)
     kv[y_hi, 0:192, mine] = kv_out[h]
     loaded("q")
+    for load in loads["p"] + loads["o"]:
+        load.start()
     rows = (matmul(normed[...], wq[...]) * (LOG2E / math.sqrt(HEAD_DIM))).T.astype(bf)
     for i in range(HEADS):
         q_out[i] = rows[i * 96 : i * 96 + 96, :]
@@ -185,11 +189,18 @@
     arrive(q_away)
     own_rows = pl.ds(pl.multiple_of(p * BLOCK, BLOCK), BLOCK)
     cots[own_rows, :] = cot_ref[...]
-    cot_copies = [
-        remote(cot_ref, cots.at[own_rows], s_send.at[k], s_recv.at[k], dev(z, plane(0, k), c))
-        for k in range(1, 4)
-    ]
-    cot_copies.append(remote(cot_ref, cots.at[own_rows], s_send.at[0], s_recv.at[0], sibling))
+    ahead, behind = dev(z, plane(0, 1), c), dev(z, plane(0, 3), c)
+
+    def cot_rows(step, first=0, count=BLOCK):
+        start = ((x + step) % 4 * 2 + c) * BLOCK + first
+        return cots.at[pl.ds(pl.multiple_of(start, 64), count)]
+
+    def cot_send(i, src, to):
+        return remote(src, src, s_send.at[i], s_recv.at[i], to)
+
+    cot_ahead = cot_send(0, cot_rows(0), ahead)
+    cot_behind = cot_send(1, cot_rows(0), behind)
+    cot_relays = [cot_send(2, cot_rows(0), sibling)]
     attend(AWAY, (OWN, NEAR), (SIB, NEAR))
     sib_a.wait_recv()
     attend_both((OWN, AWAY), (SIB, AWAY))
@@ -211,14 +222,12 @@
     z2_a.wait_recv()
     sz2_a = forward(Z2, AWAY, sibling, SIB_Z2)
     arrive([szm_a, szp_a])
+    cot_ahead.wait_recv()
+    cot_first = cot_send(3, cot_rows(3, 0, 64), ahead)
+    cot_behind.wait_recv()
+    cot_second = cot_send(4, cot_rows(1, 64, 64), behind)
+    cot_relays += [cot_send(5, cot_rows(3), sibling), cot_send(6, cot_rows(1), sibling)]
     attend_both((SIB_ZM, AWAY), (SIB_ZP, AWAY), (Z2, NEAR), (Z2, AWAY))
-    arrive(cot_copies)
-    cot_relays = []
-    for k in range(1, 4):
-        rows = pl.ds(pl.multiple_of((plane(0, k, -1) % 4 * 2 + c) * BLOCK, BLOCK), BLOCK)
-        cot_relays.append(
-            remote(cots.at[rows], cots.at[rows], s_send.at[3 + k], s_recv.at[3 + k], sibling)
-        )
     arrive([sz2_n, sz2_a])
     band = pl.ds(pl.multiple_of(h * 96, 96), 96)
 
@@ -250,7 +259,6 @@
     for l in range(12):
         hhat[l] = standard[:, l * 128 : l * 128 + 128]
         ci[l, 16:144, :] = conv_in[:, l * 128 : l * 128 + 128].astype(f32)
-    sums[480:512, :] = jnp.zeros((32, 128), f32)
 
     def place_halo(ref, slot):
         low = jnp.where(s > 0, halo[slot].astype(f32), 0.0)
@@ -280,6 +288,8 @@
         return carry
 
     lax.fori_loop(0, 12, middle, 0)
+    arrive([cot_first, cot_second])
+    cot_relays.append(cot_send(7, cot_rows(2), sibling))
     arrive(halos)
     place_halo(ci, 0)
 
@@ -294,7 +304,24 @@
         dz[l, 16:144, :] = back[l] * (sig * (1.0 + value * (1.0 - sig)))
         return carry
 
-    lax.fori_loop(0, 12, activate, 0)
+    own_lanes = pl.ds(pl.multiple_of(p * 128, 128), 128)
+    act_copies = []
+
+    def send_act(i):
+        for to in range(8):
+            starts = [24 * (8 * b + to) for b in range(4 * i, 4 * i + 4)]
+            pieces = [act_t[start : start + 24, :] for start in starts]
+            act_out[i, to] = jnp.concatenate(pieces, axis=0).astype(bf)
+        act_copies.append([
+            remote(act_out.at[i, (p + k) % 8], act_in.at[i, :, own_lanes],
+                   a_send.at[7 * i + k - 1], a_recv.at[7 * i + k - 1], group[k - 1])
+            for k in range(1, 8)
+        ])
+        act_in[i, :, own_lanes] = act_out[i, p]
+
+    lax.fori_loop(0, 6, activate, 0)
+    send_act(0)
+    lax.fori_loop(6, 12, activate, 0)
     for l in range(12):
         edge[2, :, l * 128 : l * 128 + 128] = dz[l, 128:144, :].astype(bf)
         edge[3, :, l * 128 : l * 128 + 128] = dz[l, 16:32, :].astype(bf)
@@ -302,39 +329,69 @@
         remote(edge.at[2], halo.at[2], e_send.at[2], e_recv.at[2], right),
         remote(edge.at[3], halo.at[3], e_send.at[3], e_recv.at[3], left),
     ]
-    for i in range(8):
-        pieces = [act_t[24 * (8 * b + i) : 24 * (8 * b + i) + 24, :] for b in range(8)]
-        act_out[i] = jnp.concatenate(pieces, axis=0).astype(bf)
-    own_lanes = pl.ds(pl.multiple_of(p * 128, 128), 128)
-    act_copies = [
-        remote(act_out.at[(p + k) % 8], act_in.at[:, own_lanes],
-               a_send.at[k - 1], a_recv.at[k - 1], group[k - 1])
-        for k in range(1, 8)
-    ]
-    act_in[:, own_lanes] = act_out[p]
+    send_act(1)
 
     def taps_grad(l, carry):
         grad = dz[l, 16:144, :]
-        for j0 in range(0, KER, 8):
+        for j0 in range(0, KER, 16):
             rows = [
                 jnp.sum(grad * ci[l, j : j + BLOCK, :], axis=0, keepdims=True)
-                for j in range(j0, j0 + 8)
+                for j in range(j0, j0 + 16)
             ]
-            sums[pl.ds(pl.multiple_of(l * 40 + j0, 8), 8), :] = jnp.concatenate(rows, axis=0)
+            at = pl.ds(pl.multiple_of(l * KER + j0, 16), 16)
+            b_out[at, :] = jnp.concatenate(rows, axis=0).astype(bf)
         return carry
 
     lax.fori_loop(0, 12, taps_grad, 0)
+    share = 12 * KER // 8
+
+    def share_of(i):
+        return pl.ds(pl.multiple_of(i * share, share), share)
+
+    b_copies = [
+        remote(b_out.at[share_of((p + k) % 8)], b_in.at[k - 1],
+               b_send.at[k - 1], b_recv.at[k - 1], group[k - 1])
+        for k in range(1, 8)
+    ]
+
+    t_copies = []
+
+    def tile_rows(i):
+        arrive(act_copies[i])
+        for j in range(2):
+            tile = matmul(act_in[i], cots[:, j * 768 : j * 768 + 768])
+            for b in range(2):
+                tile_out[j, 2 * i + b] = tile[48 * b : 48 * b + 48, :].astype(bf)
+            for b in range(2):
+                to = 2 * i + b
+                sent = pltpu.make_async_remote_copy(
+                    src_ref=tile_out.at[j, to], dst_ref=tile_in.at[j, z],
+                    send_sem=t_send.at[4 * j + to], recv_sem=t_recv.at[4 * j + z],
+                    device_id=dev(to, h, c), device_id_type=pl.DeviceIdType.MESH,
+                )
+                t_copies.append((to, sent))
+
+                @pl.when(z != to)
+                def _():
+                    sent.start()
+
+    arrive(cot_relays)
+    tile_rows(0)
+    arrive(b_copies)
+    c_in[z] = sum([b_out[share_of(p), :].astype(f32)] + [b_in[k].astype(f32) for k in range(7)]).astype(bf)
+    c_copies = [
+        remote(c_in.at[z], c_in.at[z], c_send.at[k], c_recv.at[k], z_peers[k]) for k in range(3)
+    ]
+    tile_rows(1)
 
     arrive(halos)
     place_halo(dz, 2)
     part[...] = jnp.zeros_like(part)
+    gain_sum[...] = jnp.zeros_like(gain_sum)
 
     def backward(l, carry):
         grad = grad_rows(l, 0, BLOCK)
-        row = jnp.sum(grad * hhat[l], axis=0, keepdims=True)
-        sums[pl.ds(pl.multiple_of(l * 40 + 32, 8), 8), :] = jnp.concatenate(
-            [row, jnp.zeros((7, 128), f32)], axis=0
-        )
+        gain_sum[pl.ds(l, 1), :] = jnp.sum(grad * hhat[l], axis=0, keepdims=True)
         g = grad * gain_conv_ref[span_of(l)].reshape(1, 128)
         back[l] = g
         part[0] += g
@@ -342,32 +399,15 @@
         return carry
 
     lax.fori_loop(0, 12, backward, 0)
-    b_out[...] = sums[...].astype(bf)
-    b_copies = [
-        remote(b_out.at[pl.ds(pl.multiple_of((p + k) % 8 * 64, 64), 64)], b_in.at[k - 1],
-               b_send.at[k - 1], b_recv.at[k - 1], group[k - 1])
-        for k in range(1, 8)
-    ]
-
-    arrive(act_copies)
-    arrive(cot_relays)
-    t_copies = []
-    for i in range(2):
-        tile = matmul(act_in[...], cots[:, i * 768 : i * 768 + 768])
-        for b in range(4):
-            tile_out[i, b] = tile[48 * b : 48 * b + 48, :].astype(bf)
-        t_copies.append([
-            remote(tile_out.at[i, (z + k) % 4], tile_in.at[i, k - 1],
-                   t_send.at[3 * i + k - 1], t_recv.at[3 * i + k - 1], z_peers[k - 1])
-            for k in range(1, 4)
-        ])
-    arrive(b_copies)
-    own = pl.ds(pl.multiple_of(p * 64, 64), 64)
-    c_in[z] = (sums[own, :] + sum(b_in[k].astype(f32) for k in range(7))).astype(bf)
-    c_copies = [
-        remote(c_in.at[z], c_in.at[z], c_send.at[k], c_recv.at[k], z_peers[k]) for k in range(3)
-    ]
-    out_ref[...] = (hidden[...].astype(f32) + matmul(act[...], wp[...])).astype(bf)
+
+    def spread(ref, at, base, peers, value):
+        ref[at] = value
+        return [
+            remote(ref.at[at], ref.at[at], n_send.at[base + k], n_recv.at[base + k], to)
+            for k, to in enumerate(peers)
+        ]
+
+    n_copies = spread(n_group, p, 0, group, gain_sum[...])
     arrive(c_copies)
     d_in[y] = sum(c_in[k].astype(f32) for k in range(4)).astype(bf)
     d_copies = [
@@ -378,12 +418,38 @@
     for l in range(12):
         cut = slice(l * 128, l * 128 + 128)
         inner = back[l] - mean_g - hhat[l] * mean_gh
-        gh_ref[:, cut] = (cot_ref[:, cut].astype(f32) + rstd * inner).astype(bf)
+        gh_rows[:, cut] = (cot_ref[:, cut].astype(f32) + rstd * inner).astype(bf)
+    gh_store = pltpu.make_async_copy(gh_rows, gh_ref, o_sem.at[0])
+    gh_store.start()
+    arrive(n_copies)
+    n_copies = spread(n_z, z, 7, z_peers, sum(n_group[k] for k in range(8)))
+    arrive(d_copies)
+    total[share_of(p), :] = sum(d_in[k].astype(f32) for k in range(4)).astype(bf)
+    g_copies = [
+        remote(total.at[share_of(p)], total.at[share_of(p)], g_send.at[k], g_recv.at[k], group[k])
+        for k in range(7)
+    ]
+    out_rows[...] = (hidden[...].astype(f32) + matmul(act[...], wp[...])).astype(bf)
+    out_store = pltpu.make_async_copy(out_rows, out_ref, o_sem.at[1])
+    out_store.start()
+    arrive(n_copies)
+    n_copies = spread(n_y, y, 10, y_peers, sum(n_z[k] for k in range(4)))
     y_copies = []
 
     def along_y(i):
-        arrive(t_copies[i])
-        mixed = tile_out[i, z].astype(f32) + sum(tile_in[i, k].astype(f32) for k in range(3))
+        for k in range(4):
+            got = pltpu.make_async_remote_copy(
+                src_ref=tile_out.at[i, k], dst_ref=tile_in.at[i, k],
+                send_sem=t_send.at[4 * i + k], recv_sem=t_recv.at[4 * i + k],
+                device_id=dev(k, h, c), device_id_type=pl.DeviceIdType.MESH,
+            )
+
+            @pl.when(z != k)
+            def _():
+                got.wait_recv()
+
+        tile_in[i, z] = tile_out[i, z]
+        mixed = sum(tile_in[i, k].astype(f32) for k in range(4))
         for b in range(2):
             rows = mixed[24 * b : 24 * b + 24, :]
             y_out[i, b] = jnp.concatenate([rows[:, :384], rows[:, 384:]], axis=0).astype(bf)
@@ -395,24 +461,28 @@
         y_in[i, y] = y_out[i, y_hi]
 
     along_y(0)
-    arrive(d_copies)
-    total[own, :] = sum(d_in[k].astype(f32) for k in range(4)).astype(bf)
-    g_copies = [
-        remote(total.at[own], total.at[own], g_send.at[k], g_recv.at[k], group[k])
-        for k in range(7)
-    ]
     along_y(1)
     scale = 1.0 / math.sqrt(2 * 64 * BLOCK)
+    arrive(g_copies)
+    arrive(n_copies)
+    gain_total = sum(n_y[k] for k in range(4)) * scale
+    for l in range(12):
+        cut = slice(l * 128, l * 128 + 128)
+        gk_ref[:, cut] = total[l * KER : l * KER + KER, :].astype(f32) * scale
+        gg_ref[:, cut] = gain_total[l : l + 1, :]
     for i in range(2):
         arrive(y_copies[i])
         whole = sum(y_in[i, k].astype(f32) for k in range(4)) * scale
         gp_ref[:, i * 768 : i * 768 + 384] = whole[:24, :]
         gp_ref[:, i * 768 + 384 : i * 768 + 768] = whole[24:, :]
-    arrive(g_copies)
-    for l in range(12):
-        cut = slice(l * 128, l * 128 + 128)
-        gk_ref[:, cut] = total[l * 40 : l * 40 + 32, :].astype(f32) * scale
-        gg_ref[:, cut] = total[l * 40 + 32 : l * 40 + 40, :].astype(f32)[:1, :] * scale
+    gh_store.wait()
+    out_store.wait()
+    for to, sent in t_copies:
+
+        @pl.when(z != to)
+        def _():
+            sent.wait_send()
+
     for copy in copies:
         copy.wait_send()
 
@@ -442,18 +512,21 @@
         ((96, 1024), bf), ((WIDE, 128), bf), ((8 * BLOCK, D), bf),
         ((BLOCK, D), bf), ((12, BLOCK, 128), f32), ((12, 160, 128), f32), ((12, BLOCK, 128), f32),
         ((12, 160, 128), f32), ((12, BLOCK, 128), f32), ((BLOCK, D), bf), ((D, BLOCK), f32),
-        ((8, 192, 128), bf), ((192, 1024), bf), ((4, 16, D), bf), ((4, 16, D), bf),
-        ((2, 4, 48, 768), bf), ((2, 3, 48, 768), bf), ((2, 2, 48, 384), bf), ((2, 4, 48, 384), bf),
-        ((2, BLOCK, 128), f32), ((512, 128), f32), ((512, 128), bf), ((7, 64, 128), bf),
-        ((4, 64, 128), bf), ((4, 64, 128), bf), ((512, 128), bf),
-    ]
-    counts = [10, 8, 8, 8, 8, 8, 8, 14, 14, 7, 7, 4, 4, 7, 7, 7, 7, 3, 3, 3, 3, 7, 7, 6, 6, 6, 6]
+        ((2, 8, 96, 128), bf), ((2, 96, 1024), bf), ((4, 16, D), bf), ((4, 16, D), bf),
+        ((2, 4, 48, 768), bf), ((2, 4, 48, 768), bf), ((2, 2, 48, 384), bf), ((2, 4, 48, 384), bf),
+        ((2, BLOCK, 128), f32), ((16, 128), f32), ((384, 128), bf), ((7, 48, 128), bf),
+        ((4, 48, 128), bf), ((4, 48, 128), bf), ((384, 128), bf),
+        ((8, 16, 128), f32), ((4, 16, 128), f32), ((4, 16, 128), f32),
+        ((BLOCK, D), bf), ((BLOCK, D), bf),
+    ]
+    counts = [10, 8, 8, 8, 8, 8, 8, 14, 14, 8, 8, 4, 4, 14, 14, 7, 7, 3, 3, 3, 3, 7, 7, 8, 8, 6, 6]
+    counts += [13, 13, 2]
     results = pl.pallas_call(
         layer_kernel,
         name="layer",
         out_shape=tuple(outs + [jax.ShapeDtypeStruct((1, D), f32)]),
         in_specs=[vmem, vmem, hbm, hbm, hbm, hbm, vmem, vmem, hbm, vmem],
-        out_specs=(vmem,) * 5,
+        out_specs=(hbm, hbm, vmem, vmem, vmem),
         scratch_shapes=[pltpu.VMEM(*shape) for shape in scratch] + [dma((n,)) for n in counts],
         compiler_params=pltpu.CompilerParams(
             collective_id=0, has_side_effects=True, vmem_limit_bytes=60 << 20

time: 82.8 us -> 76.3 us (0.921)
  Pallas kernels: 81.8 us -> 74.6 us
    pallas_call x1, Pallas kernels: 78.9 us -> 71.8 us  [layer(): pl.pallas_call(layer_kernel, name='layer', out_shape=tuple(outs + [jax.Sh...]
where the time goes in v5:
time: 76.3 us; the launch traced here: 75.4 us
  Pallas kernels  74.6 us (98%)
  between operations  0.8 us (1%)
    pallas_call x1, Pallas kernels, layer(): pl.pallas_call(layer_kernel, name='layer', out_shape=tuple(outs + [jax.Sh...  71.8 us
    pallas_call x1, Pallas kernels, layer(): pl.pallas_call(finish_kernel, name='finish', out_shape=tuple(outs + [jax....  2.85 us

profile of v5, /device:TPU:1, one launch (start us, length us, event | category | flops | bytes accessed | tf_op | source)
XLA Modules:
  0.0 75.4 jit_solution(13971226727222180615)
XLA Ops:
  0.6 71.8 %layer.1 = (bf16[128,1536]{1,0:T(8,128)(2,1)}, bf16[128,1536]{1,0:T(8,128)(2,1)}, f32[24,1536]{1,0:T(8,128)}, f32[32,1536]{1,0:T(8,128)}, f32[1,1536]{1,0:T(1,128)}) custom-call(bf16[128,1536]{1,0:T(8,128)(2,1)} %bitcast.4, f32[1536]{0:T(1024)} %gain_ref.1, bf16[1536,768]{1,0:T(8,128)(2,1)} %wk_hbm.1, bf16[1536,768]{1,0:T(8,128)(2,1)} %wv_hbm.1, ...), custom_call_target="tpu_custom_call" | custom-call | flops 8999999488 | bytes 16777216 | tf_op jit(solution)/shard_map/layer/pallas_call | solution.py:524
  72.4 2.9 %finish.1 = (bf16[128,1536]{1,0:T(8,128)(2,1)}, bf16[128,1536]{1,0:T(8,128)(2,1)}, f32[24,1536]{1,0:T(8,128)}, f32[32,1536]{1,0:T(8,128)}, f32[1536]{0:T(1024)}) custom-call(bf16[128,1536]{1,0:T(8,128)(2,1)} %get-tuple-element.15.out, bf16[128,1536]{1,0:T(8,128)(2,1)} %get-tuple-element.16.gh, f32[24,1536]{1,0:T(8,128)} %get-tuple-element.17.gp, ...), custom_call_target="tpu_custom_call" | custom-call | tf_op jit(solution)/shard_map/finish/pallas_call | solution.py:538

commit v6 on v5

--- a/solution.py
+++ b/solution.py
@@ -354,6 +354,13 @@
         for k in range(1, 8)
     ]
 
+    def spread(ref, at, base, peers, value):
+        ref[at] = value
+        return [
+            remote(ref.at[at], ref.at[at], n_send.at[base + k], n_recv.at[base + k], to)
+            for k, to in enumerate(peers)
+        ]
+
     t_copies = []
 
     def tile_rows(i):
@@ -375,6 +382,35 @@
                 def _():
                     sent.start()
 
+    y_copies = []
+
+    def along_y(i):
+        for k in range(4):
+            got = pltpu.make_async_remote_copy(
+                src_ref=tile_out.at[i, k], dst_ref=tile_in.at[i, k],
+                send_sem=t_send.at[4 * i + k], recv_sem=t_recv.at[4 * i + k],
+                device_id=dev(k, h, c), device_id_type=pl.DeviceIdType.MESH,
+            )
+
+            @pl.when(z != k)
+            def _():
+                got.wait_recv()
+
+        tile_in[i, z] = tile_out[i, z]
+        mixed = sum(tile_in[i, k].astype(f32) for k in range(4))
+        for b in range(2):
+            rows = mixed[24 * b : 24 * b + 24, :]
+            y_out[i, b] = jnp.concatenate([rows[:, :384], rows[:, 384:]], axis=0).astype(bf)
+        y_copies.append([
+            remote(y_out.at[i, (y + k) % 4 // 2], y_in.at[i, y],
+                   y_send.at[3 * i + k - 1], y_recv.at[3 * i + k - 1], y_peers[k - 1])
+            for k in range(1, 4)
+        ])
+        y_in[i, y] = y_out[i, y_hi]
+
+    out_rows[...] = (hidden[...].astype(f32) + matmul(act[...], wp[...])).astype(bf)
+    out_store = pltpu.make_async_copy(out_rows, out_ref, o_sem.at[1])
+    out_store.start()
     arrive(cot_relays)
     tile_rows(0)
     arrive(b_copies)
@@ -383,7 +419,6 @@
         remote(c_in.at[z], c_in.at[z], c_send.at[k], c_recv.at[k], z_peers[k]) for k in range(3)
     ]
     tile_rows(1)
-
     arrive(halos)
     place_halo(dz, 2)
     part[...] = jnp.zeros_like(part)
@@ -399,13 +434,6 @@
         return carry
 
     lax.fori_loop(0, 12, backward, 0)
-
-    def spread(ref, at, base, peers, value):
-        ref[at] = value
-        return [
-            remote(ref.at[at], ref.at[at], n_send.at[base + k], n_recv.at[base + k], to)
-            for k, to in enumerate(peers)
-        ]
 
     n_copies = spread(n_group, p, 0, group, gain_sum[...])
     arrive(c_copies)
@@ -429,38 +457,9 @@
         remote(total.at[share_of(p)], total.at[share_of(p)], g_send.at[k], g_recv.at[k], group[k])
         for k in range(7)
     ]
-    out_rows[...] = (hidden[...].astype(f32) + matmul(act[...], wp[...])).astype(bf)
-    out_store = pltpu.make_async_copy(out_rows, out_ref, o_sem.at[1])
-    out_store.start()
+    along_y(0)
     arrive(n_copies)
     n_copies = spread(n_y, y, 10, y_peers, sum(n_z[k] for k in range(4)))
-    y_copies = []
-
-    def along_y(i):
-        for k in range(4):
-            got = pltpu.make_async_remote_copy(
-                src_ref=tile_out.at[i, k], dst_ref=tile_in.at[i, k],
-                send_sem=t_send.at[4 * i + k], recv_sem=t_recv.at[4 * i + k],
-                device_id=dev(k, h, c), device_id_type=pl.DeviceIdType.MESH,
-            )
-
-            @pl.when(z != k)
-            def _():
-                got.wait_recv()
-
-        tile_in[i, z] = tile_out[i, z]
-        mixed = sum(tile_in[i, k].astype(f32) for k in range(4))
-        for b in range(2):
-            rows = mixed[24 * b : 24 * b + 24, :]
-            y_out[i, b] = jnp.concatenate([rows[:, :384], rows[:, 384:]], axis=0).astype(bf)
-        y_copies.append([
-            remote(y_out.at[i, (y + k) % 4 // 2], y_in.at[i, y],
-                   y_send.at[3 * i + k - 1], y_recv.at[3 * i + k - 1], y_peers[k - 1])
-            for k in range(1, 4)
-        ])
-        y_in[i, y] = y_out[i, y_hi]
-
-    along_y(0)
     along_y(1)
     scale = 1.0 / math.sqrt(2 * 64 * BLOCK)
     arrive(g_copies)

time: 76.3 us -> 75.5 us (0.990)
  no operation moved by 1% of the time
where the time goes in v6:
time: 75.5 us; the launch traced here: 74.7 us
  Pallas kernels  73.9 us (98%)
  between operations  0.8 us (1%)
    pallas_call x1, Pallas kernels, layer(): pl.pallas_call(layer_kernel, name='layer', out_shape=tuple(outs + [jax.Sh...  71 us
    pallas_call x1, Pallas kernels, layer(): pl.pallas_call(finish_kernel, name='finish', out_shape=tuple(outs + [jax....  2.85 us

profile of v6, /device:TPU:1, one launch (start us, length us, event | category | flops | bytes accessed | tf_op | source)
XLA Modules:
  0.0 74.7 jit_solution(6367369294369159565)
XLA Ops:
  0.6 71.0 %layer.1 = (bf16[128,1536]{1,0:T(8,128)(2,1)}, bf16[128,1536]{1,0:T(8,128)(2,1)}, f32[24,1536]{1,0:T(8,128)}, f32[32,1536]{1,0:T(8,128)}, f32[1,1536]{1,0:T(1,128)}) custom-call(bf16[128,1536]{1,0:T(8,128)(2,1)} %bitcast.4, f32[1536]{0:T(1024)} %gain_ref.1, bf16[1536,768]{1,0:T(8,128)(2,1)} %wk_hbm.1, bf16[1536,768]{1,0:T(8,128)(2,1)} %wv_hbm.1, ...), custom_call_target="tpu_custom_call" | custom-call | flops 8999999488 | bytes 16777216 | tf_op jit(solution)/shard_map/layer/pallas_call | solution.py:523
  71.7 2.9 %finish.1 = (bf16[128,1536]{1,0:T(8,128)(2,1)}, bf16[128,1536]{1,0:T(8,128)(2,1)}, f32[24,1536]{1,0:T(8,128)}, f32[32,1536]{1,0:T(8,128)}, f32[1536]{0:T(1024)}) custom-call(bf16[128,1536]{1,0:T(8,128)(2,1)} %get-tuple-element.15.out, bf16[128,1536]{1,0:T(8,128)(2,1)} %get-tuple-element.16.gh, f32[24,1536]{1,0:T(8,128)} %get-tuple-element.17.gp, ...), custom_call_target="tpu_custom_call" | custom-call | tf_op jit(solution)/shard_map/finish/pallas_call | solution.py:537

commit v7 on v6

--- a/solution.py
+++ b/solution.py
@@ -31,12 +31,12 @@
 
 
 def layer_kernel(
-    x_ref, gain_ref, wk_hbm, wv_hbm, wq_hbm, wo_hbm, gain_conv_ref, taps_ref, wp_hbm, cot_ref,
+    x_ref, gain_ref, wk_hbm, wv_hbm, wq_hbm, wo_hbm, gain_conv_ref, taps_hbm, wp_hbm, cot_hbm,
     out_ref, gh_ref, gp_ref, gk_ref, gg_ref,
     wk, wv, wq, wo, wp, normed, kv_out, q_out, kv, qt, acc, top, mix_out, mixt, cots,
     hidden, hhat, ci, back, dz, conv, act, act_t, act_out, act_in, edge, halo, tile_out, tile_in,
     y_out, y_in, part, gain_sum, b_out, b_in, c_in, d_in, total, n_group, n_z, n_y,
-    gh_rows, out_rows,
+    gh_rows, out_rows, taps_ref,
     w_sem, kv_send, kv_recv, q_send, q_recv, m_send, m_recv, r_send, r_recv, s_send, s_recv,
     e_send, e_recv, a_send, a_recv, b_send, b_recv, c_send, c_recv, d_send, d_recv,
     g_send, g_recv, t_send, t_recv, y_send, y_recv, n_send, n_recv, o_sem,
@@ -92,6 +92,12 @@
                 loads[name][-1].start()
             sem += 1
 
+    own_rows = pl.ds(pl.multiple_of(p * BLOCK, BLOCK), BLOCK)
+    late_loads = [
+        pltpu.make_async_copy(cot_hbm, cots.at[own_rows], o_sem.at[2]),
+        pltpu.make_async_copy(taps_hbm, taps_ref, o_sem.at[3]),
+    ]
+
     def loaded(name):
         for load in loads[name]:
             load.wait()
@@ -129,7 +135,7 @@
     kv_away = exchange(lambda i: kv_out.at[i], kv.at[y_hi, 0:192, mine], kv_send, kv_recv, away)
     kv[y_hi, 0:192, mine] = kv_out[h]
     loaded("q")
-    for load in loads["p"] + loads["o"]:
+    for load in late_loads + loads["p"] + loads["o"]:
         load.start()
     rows = (matmul(normed[...], wq[...]) * (LOG2E / math.sqrt(HEAD_DIM))).T.astype(bf)
     for i in range(HEADS):
@@ -176,7 +182,9 @@
     zp_n = forward(OWN, NEAR, down, ZP)
     sib_n = forward(OWN, NEAR, sibling, SIB)
     loaded("p")
-    grads = matmul(cot_ref[...], wp[...], 1, 1)
+    for load in late_loads:
+        load.wait()
+    grads = matmul(cots[own_rows, :], wp[...], 1, 1)
     for l in range(12):
         back[l] = grads[:, l * 128 : l * 128 + 128]
     arrive(kv_away)
@@ -187,8 +195,6 @@
     sib_n.wait_recv()
     attend(NEAR, (OWN, NEAR), (SIB, NEAR))
     arrive(q_away)
-    own_rows = pl.ds(pl.multiple_of(p * BLOCK, BLOCK), BLOCK)
-    cots[own_rows, :] = cot_ref[...]
     ahead, behind = dev(z, plane(0, 1), c), dev(z, plane(0, 3), c)
 
     def cot_rows(step, first=0, count=BLOCK):
@@ -446,7 +452,7 @@
     for l in range(12):
         cut = slice(l * 128, l * 128 + 128)
         inner = back[l] - mean_g - hhat[l] * mean_gh
-        gh_rows[:, cut] = (cot_ref[:, cut].astype(f32) + rstd * inner).astype(bf)
+        gh_rows[:, cut] = (cots[own_rows, cut].astype(f32) + rstd * inner).astype(bf)
     gh_store = pltpu.make_async_copy(gh_rows, gh_ref, o_sem.at[0])
     gh_store.start()
     arrive(n_copies)
@@ -516,15 +522,15 @@
         ((2, BLOCK, 128), f32), ((16, 128), f32), ((384, 128), bf), ((7, 48, 128), bf),
         ((4, 48, 128), bf), ((4, 48, 128), bf), ((384, 128), bf),
         ((8, 16, 128), f32), ((4, 16, 128), f32), ((4, 16, 128), f32),
-        ((BLOCK, D), bf), ((BLOCK, D), bf),
+        ((BLOCK, D), bf), ((BLOCK, D), bf), ((KER, D), f32),
     ]
     counts = [10, 8, 8, 8, 8, 8, 8, 14, 14, 8, 8, 4, 4, 14, 14, 7, 7, 3, 3, 3, 3, 7, 7, 8, 8, 6, 6]
-    counts += [13, 13, 2]
+    counts += [13, 13, 4]
     results = pl.pallas_call(
         layer_kernel,
         name="layer",
         out_shape=tuple(outs + [jax.ShapeDtypeStruct((1, D), f32)]),
-        in_specs=[vmem, vmem, hbm, hbm, hbm, hbm, vmem, vmem, hbm, vmem],
+        in_specs=[vmem, vmem, hbm, hbm, hbm, hbm, vmem, hbm, hbm, hbm],
         out_specs=(hbm, hbm, vmem, vmem, vmem),
         scratch_shapes=[pltpu.VMEM(*shape) for shape in scratch] + [dma((n,)) for n in counts],
         compiler_params=pltpu.CompilerParams(

time: 75.5 us -> 75.3 us (level)
  no operation moved by 1% of the time
where the time goes in v7:
time: 75.3 us; the launch traced here: 74.4 us
  Pallas kernels  73.6 us (98%)
  between operations  0.8 us (1%)
    pallas_call x1, Pallas kernels, layer(): pl.pallas_call(layer_kernel, name='layer', out_shape=tuple(outs + [jax.Sh...  70.7 us
    pallas_call x1, Pallas kernels, layer(): pl.pallas_call(finish_kernel, name='finish', out_shape=tuple(outs + [jax....  2.85 us

profile of v7, /device:TPU:1, one launch (start us, length us, event | category | flops | bytes accessed | tf_op | source)
XLA Modules:
  0.0 74.4 jit_solution(7058406866087379297)
XLA Ops:
  0.6 70.7 %layer.1 = (bf16[128,1536]{1,0:T(8,128)(2,1)}, bf16[128,1536]{1,0:T(8,128)(2,1)}, f32[24,1536]{1,0:T(8,128)}, f32[32,1536]{1,0:T(8,128)}, f32[1,1536]{1,0:T(1,128)}) custom-call(bf16[128,1536]{1,0:T(8,128)(2,1)} %bitcast.4, f32[1536]{0:T(1024)} %gain_ref.1, bf16[1536,768]{1,0:T(8,128)(2,1)} %wk_hbm.1, bf16[1536,768]{1,0:T(8,128)(2,1)} %wv_hbm.1, ...), custom_call_target="tpu_custom_call" | custom-call | flops 8999999488 | bytes 16777216 | tf_op jit(solution)/shard_map/layer/pallas_call | solution.py:529
  71.4 2.9 %finish.1 = (bf16[128,1536]{1,0:T(8,128)(2,1)}, bf16[128,1536]{1,0:T(8,128)(2,1)}, f32[24,1536]{1,0:T(8,128)}, f32[32,1536]{1,0:T(8,128)}, f32[1536]{0:T(1024)}) custom-call(bf16[128,1536]{1,0:T(8,128)(2,1)} %get-tuple-element.15.out, bf16[128,1536]{1,0:T(8,128)(2,1)} %get-tuple-element.16.gh, f32[24,1536]{1,0:T(8,128)} %get-tuple-element.17.gp, ...), custom_call_target="tpu_custom_call" | custom-call | tf_op jit(solution)/shard_map/finish/pallas_call | solution.py:543
